TPU v7x, 256 devices: a whole 4x4x8 slice. The times are simulated.
256 devices in a mesh: member: 4 (over z_lo), space: 64 (over z_hi, y, x, core).
Axes of the slice: x: 4, y: 4, z: 8 (z_hi: 2, z_lo: 4; z = z_hi * 4 + z_lo), core: 2. Of those that a mesh axis runs over, the one named last changes fastest.
Arguments:
- tracers: float32 [8, 48, 8, 512, 128], P('member', None, None, 'space'), may hold values from -6 to 6
- horiz_mix: float32 [8, 512, 128], P(None, 'space'), may hold values from 0.05 to 0.22
- vert_mix: float32 [7, 512, 128], P(None, 'space'), may hold values from 0.02 to 0.2
- sunlit: int32 [512], replicated, may hold values from 0 to 1, as said below
- interaction: float32 [48, 48], replicated, may hold values from -0.875 to 0.875
- remin: float32 [48], replicated, may hold values from 0.05 to 0.3
- obs_cell: int32 [4096], replicated, may hold values from 0 to 65535, as said below
- obs_tile: int32 [4096], replicated, may hold values from 0 to 63
- obs_value: float32 [4096], replicated, may hold values from -6 to 6
- obs_noise: float32 [8, 4096], replicated, may hold values from -5 to 5
- obs_var: float32 [4096], replicated, may hold values from 0.25 to 1
Outputs:
- analysis: float32 [8, 48, 8, 512, 128], P('member', None, None, 'space')
Inputs may be any that keep to these rules, and one draw needn't show every extreme that they name: The sunlit rows are exactly those of half of the tiles, cyclically consecutive; each tile is wholly sunlit or wholly dark. `obs_cell`: an observation may lie in any tile; every tile uses at least one observation that lies in the tile 64 / 2 tiles on, counted round.
All inputs are finite; a program needn't handle non-finite values.
Results may differ from a plain program's by a relative error of at most 0.0003.
Values sent between devices are 32-bit elements; how exact they have to be, the bound alone decides.
A program may use at most 64 MiB of HBM per device.

v0:
```python
import jax
import jax.numpy as jnp
from jax import lax
from jax.sharding import PartitionSpec as P

NSUB = 4


def padded_2(value, sides, width):
    for axis, dim in sides:
        count, length = (lax.axis_size(axis), value.shape[dim])
        up = [(i, (i + 1) % count) for i in range(count - 1)]
        down = [(j, i) for i, j in up]
        last = lax.slice_in_dim(value, length - width, length, axis=dim)
        initial = lax.slice_in_dim(value, 0, width, axis=dim)
        before = lax.ppermute(last, axis, up)
        after = lax.ppermute(initial, axis, down)
        value = jnp.concatenate([before, value, after], axis=dim)
    return value


def copy_for_each(value, axis):
    count = lax.axis_size(axis)
    return lax.all_to_all(
        jnp.broadcast_to(value[None], (count, *value.shape)), axis, 0, 0, tiled=True
    )


def taken_together(value, axis):
    return copy_for_each(value, axis).sum(axis=0)


def laid_out(parts, dim):
    shape = list(parts.shape[1:])
    shape[dim] *= parts.shape[0]
    return jnp.moveaxis(parts, 0, dim).reshape(shape)


def collect(value, axis, dim):
    return laid_out(copy_for_each(value, axis), dim)


def sunlit_update(column_block, interaction, remin, light_levels):
    fraction = 1.0 / NSUB
    light_shape = (1, 1, -1) + (1,) * (column_block.ndim - 3)
    remin_shape = (1, -1) + (1,) * (column_block.ndim - 2)
    for substep in range(NSUB):
        uptake = jnp.einsum(
            "ji,mi...->mj...", interaction, column_block, precision=lax.Precision.HIGHEST
        )
        column_block = column_block + fraction * (
            light_levels.reshape(light_shape) * jnp.tanh(uptake)
            - remin.reshape(remin_shape) * column_block
        )
    return column_block


def dark_update(column_block, remin):
    fraction = 1.0 / NSUB
    remin_shape = (1, -1) + (1,) * (column_block.ndim - 2)
    for substep in range(NSUB):
        column_block = column_block - fraction * (remin.reshape(remin_shape) * column_block)
    return column_block


def ecology_block(state, flags, interaction, remin, light_levels):
    return lax.cond(
        flags[0] > 0,
        lambda value: sunlit_update(value, interaction, remin, light_levels),
        lambda value: dark_update(value, remin),
        state,
    )


def on_device(
    tracers,
    horiz_mix,
    vert_mix,
    sunlit,
    interaction,
    remin,
    obs_cell,
    obs_tile,
    obs_value,
    obs_noise,
    obs_var,
):
    pair_size = tracers.shape[0]
    row_count = tracers.shape[3]
    space_count = lax.axis_size("space")
    tile_index = lax.axis_index("space")
    member_count = pair_size * lax.axis_size("member")
    padded = padded_2(tracers, (("space", 3),), 1)
    row_ids = jnp.arange(row_count)
    north_rows = jnp.where(
        ((row_ids == 0) & (tile_index == 0))[:, None], tracers, padded[..., :-2, :]
    )
    south_rows = jnp.where(
        ((row_ids == row_count - 1) & (tile_index == space_count - 1))[:, None],
        tracers,
        padded[..., 2:, :],
    )
    west_cols = jnp.concatenate([tracers[..., :1], tracers[..., :-1]], axis=4)
    east_cols = jnp.concatenate([tracers[..., 1:], tracers[..., -1:]], axis=4)
    laplace = north_rows + south_rows + west_cols + east_cols - 4.0 * tracers
    state = tracers + horiz_mix[None, None] * laplace
    vertical_flux = vert_mix[None, None] * (state[:, :, 1:] - state[:, :, :-1])
    zero_layer = jnp.zeros_like(state[:, :, :1])
    state = (
        state
        + jnp.concatenate([vertical_flux, zero_layer], axis=2)
        - jnp.concatenate([zero_layer, vertical_flux], axis=2)
    )
    light_levels = 0.6 * jnp.exp(-0.4 * jnp.arange(state.shape[2], dtype=jnp.float32))
    own_flags = lax.dynamic_slice_in_dim(sunlit, tile_index * row_count, row_count)
    state = ecology_block(state, own_flags, interaction, remin, light_levels)
    cells_tile = row_count * state.shape[4]
    local_cell = obs_cell - tile_index * cells_tile
    inside = (local_cell >= 0) & (local_cell < cells_tile)
    surface = state[:, 0, 0].reshape(pair_size, cells_tile)
    picked = jnp.take(surface, jnp.clip(local_cell, 0, cells_tile - 1), axis=1)
    own_values = jnp.where(inside[None, :], picked, 0.0)
    pair_values = taken_together(own_values, "space")
    observed = collect(pair_values, "member", 0)
    spread = observed - jnp.mean(observed, axis=0, keepdims=True)
    innov = obs_value[None, :] + obs_noise - observed
    selection = jnp.where(obs_tile == tile_index, 1.0 / obs_var, 0.0)
    scaled = spread * selection[None, :]
    gram_matrix = (member_count - 1) * jnp.eye(member_count, dtype=jnp.float32) + jnp.dot(
        scaled, spread.T, precision=lax.Precision.HIGHEST
    )
    right_side = jnp.dot(scaled, innov.T, precision=lax.Precision.HIGHEST)
    cholesky_factor = jnp.linalg.cholesky(gram_matrix)
    weights = jax.scipy.linalg.cho_solve((cholesky_factor, True), right_side)
    centered = weights - jnp.mean(weights, axis=0, keepdims=True)
    flattened = state.reshape(pair_size, state.shape[1], state.shape[2], cells_tile)
    grouped = lax.all_to_all(flattened, "member", split_axis=3, concat_axis=0, tiled=True)
    updated = grouped + jnp.einsum(
        "kabc,km->mabc", grouped, centered, precision=lax.Precision.HIGHEST
    )
    result = lax.all_to_all(updated, "member", split_axis=0, concat_axis=3, tiled=True)
    return result.reshape(state.shape)


def solution(mesh):
    return jax.shard_map(
        on_device,
        mesh=mesh,
        in_specs=(
            P("member", None, None, "space", None),
            P(None, "space", None),
            P(None, "space", None),
            P(),
            P(),
            P(),
            P(),
            P(),
            P(),
            P(),
            P(),
        ),
        out_specs=P("member", None, None, "space", None),
        check_vma=False,
    )
```

profile of v0, /device:TPU:8, one launch (start us, length us, event | category | flops | bytes accessed | tf_op | source)
XLA Modules:
  0.0 354.8 jit_solution(9085053161751149200)
XLA Ops:
  0.0 3.7 %copy.131 = f32[2,48,8,8,128]{4,1,3,2,0:T(8,128)S(1)} copy(f32[2,48,8,8,128]{4,3,2,1,0:T(8,128)} %param.13) | data formatting | bytes 6291456 | tf_op args[0]
  3.7 0.8 fusion.54
  4.5 1.9 collective-permute-start
  6.4 5.8 %collective-permute-start.1 = (f32[2,48,8,1,128]{4,1,3,2,0:T(8,128)S(1)}, f32[2,48,8,1,128]{4,1,3,2,0:T(8,128)}, u32[]{:S(2)}, u32[]{:S(2)}) collective-permute-start(f32[2,48,8,1,128]{4,1,3,2,0:T(8,128)S(1)} %get-tuple-element.60), channel_id=1, source_target_pairs={{1,0},{2,1},{3,2},{4,3},{5,4},{6,5},{7,6},{8,7},{9,8},{10,9},{11,1... | collective-permute-start | bytes 1179656 | tf_op jit(solution)/shard_map/ppermute | solution.py:17
  12.2 3.7 %fusion.52 = (f32[2,48,8,8,127]{4,1,3,2,0:T(8,128)}, f32[2,48,8,8,127]{4,1,3,2,0:T(8,128)}) fusion(f32[2,48,8,8,128]{4,1,3,2,0:T(8,128)S(1)} %copy.131), kind=kLoop, calls=%fused_computation.83 | loop fusion | bytes 12484608 | tf_op jit(solution)/shard_map/slice | solution.py:104
  15.9 0.7 fusion.41
  16.7 1.3 compare_and_fusion
  18.0 0.8 dynamic_slice.3
  18.8 0.0 copy-start
  18.8 0.0 copy-start.4
  18.9 1.1 fusion.53
  20.0 0.0 collective-permute-done
  20.0 0.7 copy-done
  20.7 1.0 copy-done.1
  21.7 4.0 %fusion.30 = f32[2,48,8,8,128]{4,1,3,2,0:T(8,128)S(1)} fusion(f32[2,48,8,8,128]{4,1,3,2,0:T(8,128)S(1)} %copy.131, f32[2,48,8,1,128]{4,1,3,2,0:T(8,128)} %collective-permute-done.1, f32[2,48,8,1,128]{4,1,3,2,0:T(8,128)} %collective-permute-done, f32[2,48,8,8,127]{4,1,3,2,0:T(8,128)S(1)} %copy-done.1, f32[2,48,8,8,1]{4,1,3,2,0:T(8,128)S(1)} %get-tuple-element.58, ...), kind=kLoop, calls=%fused_computation.39 | loop fusion | flops 10223616 | bytes 13402128 | tf_op jit(solution)/shard_map/add | solution.py:106
  25.7 0.3 fusion.32
  26.1 0.0 copy-start.3
  26.1 0.0 copy-start.10
  26.1 0.4 pad_subtract_fusion
  26.5 0.3 copy-done.3
  26.8 18.1 %conditional.1 = (f32[2,48,8,8,128]{4,1,3,2,0:T(8,128)S(1)}) conditional(s32[]{:T(128)} %bitcast.7, (f32[48]{0:T(128)S(1)}, f32[2,48,8,8,128]{4,1,3,2,0:T(8,128)S(1)}) %tuple.31, (f32[8]{0:T(128)S(1)}, f32[8]{0:T(128)S(1)}, f32[8]{0:T(128)S(1)}, f32[8]{0:T(128)S(1)}, f32[2,48,8,8,128]{4,1,3,2,0:T(8,128)S(1)}, /*index=5*/f32[48,48]{1,0:T(8,128)S(1)}, ...), branch_computations={%region_0.1_spmd, %region_1.2_spmd} | conditional | flops 1835532288 | bytes 31494920 | solution.py:67
  27.0 2.9 fusion.20
  29.9 5.1 %fusion.5 = f32[2,48,8,8,128]{4,1,3,2,0:T(8,128)S(1)} fusion(f32[2,48,8,8,128]{4,1,3,2,0:T(8,128)S(1)} %get-tuple-element.40, f32[2,8,8,128,48]{3,4,2,1,0:T(8,128)S(1)} %fusion.20, f32[8]{0:T(128)S(1)} %get-tuple-element.53, f32[48]{0:T(128)S(1)} %get-tuple-element.43, f32[8]{0:T(128)S(1)} %get-tuple-element.54, f32[48,48]{1,0:T(8,128)S(1)} %get-tuple-element.48), kind=kOutput, calls=%fused_computation.10 | convolution fusion | flops 464781312 | bytes 9446656 | tf_op jit(solution)/shard_map/cond/branch_1_fun/ji,mi...->mj.../dot_general | solution.py:48
  35.0 2.9 fusion.17
  37.9 5.2 %fusion.1 = f32[2,48,8,8,128]{4,1,3,2,0:T(8,128)S(1)} fusion(f32[2,48,8,8,128]{4,1,3,2,0:T(8,128)S(1)} %fusion.5, f32[2,8,8,128,48]{3,4,2,1,0:T(8,128)S(1)} %fusion.17, f32[8]{0:T(128)S(1)} %get-tuple-element.51, f32[8]{0:T(128)S(1)} %get-tuple-element.52, f32[48]{0:T(128)S(1)} %get-tuple-element.43, f32[48,48]{1,0:T(8,128)S(1)} %get-tuple-element.48), kind=kOutput, calls=%fused_computation.4 | convolution fusion | flops 464781312 | bytes 9446656 | tf_op jit(solution)/shard_map/cond/branch_1_fun/ji,mi...->mj.../dot_general | solution.py:48
  44.9 1.0 copy.136
  45.9 15.2 %gather_fusion = f32[4096,2]{1,0:T(8,128)} fusion(f32[2,1024]{0,1:T(8,128)} %bitcast.89, s32[4096]{0:T(1024)S(1)} %fusion.41), kind=kCustom, calls=%fused_computation | custom fusion | bytes 81920 | tf_op jit(solution)/shard_map/jit(_take)/gather | solution.py:121
  61.2 6.0 %select_bitcast_fusion = f32[2,4096]{0,1:T(8,128)} fusion(f32[4096,2]{1,0:T(8,128)} %gather_fusion, pred[4096]{0:T(1024)(128)(4,1)S(1)} %copy-done.9, pred[4096]{0:T(1024)(128)(4,1)S(1)} %copy-done.8), kind=kLoop, calls=%fused_computation.46 | loop fusion | flops 16384 | bytes 73728 | tf_op jit(solution)/shard_map/jit(_where)/select_n | solution.py:122
  67.1 2.2 copy.137
  69.3 1.0 broadcast_in_dim.72
  70.4 57.5 %all_to_all.43 = f32[64,2,4096]{2,1,0:T(2,128)} all-to-all(f32[64,2,4096]{2,1,0:T(2,128)S(1)} %broadcast_in_dim.72), channel_id=1, replica_groups=mesh['member'=4,'space'=64] {'space'}, dimensions={0} | all-to-all | bytes 4194304 | tf_op jit(solution)/shard_map/all_to_all | solution.py:24
  127.8 2.2 reduce_sum.27
  130.1 0.7 broadcast_in_dim.73
  130.8 16.0 %all-to-all-start.2 = ((f32[4,2,4096]{2,1,0:T(2,128)}), f32[4,2,4096]{2,1,0:T(2,128)S(1)}, u32[]{:S(2)}, u32[]{:S(2)}) async-start(f32[4,2,4096]{2,1,0:T(2,128)} %broadcast_in_dim.73), calls=%async_computation.2 | async-start | bytes 262144 | tf_op jit(solution)/shard_map/all_to_all | solution.py:24
  146.8 5.0 %copy.146 = f32[2,48,8,8,128]{1,2,0,4,3:T(8,128)} copy(f32[2,48,8,8,128]{4,1,3,2,0:T(8,128)S(1)} %get-tuple-element.67) | data formatting | bytes 6291456 | tf_op jit(solution)/shard_map/reshape | solution.py:136
  151.8 10.2 %reshape.125 = f32[4,1,196608]{2,1,0:T(1,128)} reshape(f32[1024,2,8,48]{3,2,1,0:T(8,128)} %bitcast.85) | data formatting | bytes 6291456
  162.0 5.7 %all-to-all-start = ((f32[4,1,196608]{2,1,0:T(1,128)}), f32[4,1,196608]{2,1,0:T(1,128)S(1)}, u32[]{:S(2)}, u32[]{:S(2)}) async-start(f32[4,1,196608]{2,1,0:T(1,128)} %reshape.125), calls=%async_computation | async-start | bytes 6291456 | tf_op jit(solution)/shard_map/all_to_all | solution.py:137
  167.8 0.1 reduce_sum.28
  167.9 0.7 broadcast_multiply_fusion
  168.6 1.0 mul.219
  169.6 0.7 sub.77
  170.3 1.3 fusion.56
  171.6 0.1 copy.139
  171.7 0.7 cholesky.16
  172.4 0.1 select_reduce_fusion
  172.5 0.7 compare_reduce_fusion
  173.2 0.6 fusion.42
  173.8 0.6 custom-call.10
  174.4 0.1 reshape.111
  174.5 1.2 fusion.33
  175.8 0.2 fusion.43
  176.0 0.2 fusion.55
  176.2 61.8 %all-to-all-done = f32[4,1,196608]{2,1,0:T(1,128)S(1)} async-done(((f32[4,1,196608]{2,1,0:T(1,128)}), f32[4,1,196608]{2,1,0:T(1,128)S(1)}, u32[]{:S(2)}, u32[]{:S(2)}) %all-to-all-start) | async-done | bytes 3145760 | tf_op jit(solution)/shard_map/all_to_all | solution.py:137
  238.0 0.6 broadcast.223
  238.6 10.6 %reduce.7 = f32[4,196608]{1,0:T(4,128)} reduce(f32[4,1,196608]{2,1,0:T(1,128)S(1)} %all-to-all-done, f32[]{:T(128)} %broadcast.223), dimensions={1}, to_apply=%all_to_all.30.reduce_sub_computation | reduce | bytes 6291460 | tf_op jit(solution)/shard_map/all_to_all | solution.py:137
  249.2 9.0 %reshape.126 = f32[1024,2,8,48]{3,2,1,0:T(8,128)} reshape(f32[4,196608]{1,0:T(4,128)} %reduce.7) | data formatting | bytes 6291456
  258.2 6.5 %copy.147 = f32[2,48,8,4,256]{4,3,2,1,0:T(4,128)S(1)} copy(f32[2,48,8,4,256]{1,2,0,4,3:T(8,128)} %bitcast.86) | data formatting | bytes 6291456 | tf_op jit(solution)/shard_map/all_to_all | solution.py:137
  264.6 4.4 %copy.135 = f32[4,2,48,8,256]{4,1,0,3,2:T(2,128)} copy(f32[4,2,48,8,256]{4,0,3,2,1:T(4,128)S(1)} %bitcast.88) | data formatting | bytes 6291456 | tf_op jit(solution)/shard_map/all_to_all | solution.py:137
  269.0 4.1 %all_to_all.33 = f32[8,48,8,256]{3,0,2,1:T(8,128)S(1)} reshape(f32[4,2,48,8,256]{4,1,0,3,2:T(2,128)} %copy.135) | data formatting | bytes 6291456 | tf_op jit(solution)/shard_map/all_to_all | solution.py:137
  273.1 2.9 convolution_add_fusion
  276.1 1.0 copy.142
  277.1 72.7 %all_to_all.44 = f32[8,48,8,256]{3,2,1,0:T(8,128)S(1)} all-to-all(f32[8,48,8,256]{3,2,1,0:T(8,128)S(1)} %copy.142), channel_id=1, replica_groups=mesh['member'=4,'space'=64] {'member'}, dimensions={0} | all-to-all | bytes 6291456 | tf_op jit(solution)/shard_map/all_to_all | solution.py:141
  349.8 2.0 copy.143
  351.8 2.8 reshape.112
  (26 shorter events, 0.1 us)
Async XLA Ops:
  4.5 15.4 %collective-permute-start = (f32[2,48,8,1,128]{4,1,3,2,0:T(8,128)}, f32[2,48,8,1,128]{4,1,3,2,0:T(8,128)}, u32[]{:S(2)}, u32[]{:S(2)}) collective-permute-start(f32[2,48,8,1,128]{4,1,3,2,0:T(8,128)} %get-tuple-element.59), channel_id=1, source_target_pairs={{0,1},{1,2},{2,3},{3,4},{4,5},{5,6},{6,7},{7,8},{8,9},{9,10},{10,1... | collective-permute-start | bytes 1179656 | tf_op jit(solution)/shard_map/ppermute | solution.py:16
  6.4 13.5 %collective-permute-start.1 = (f32[2,48,8,1,128]{4,1,3,2,0:T(8,128)S(1)}, f32[2,48,8,1,128]{4,1,3,2,0:T(8,128)}, u32[]{:S(2)}, u32[]{:S(2)}) collective-permute-start(f32[2,48,8,1,128]{4,1,3,2,0:T(8,128)S(1)} %get-tuple-element.60), channel_id=1, source_target_pairs={{1,0},{2,1},{3,2},{4,3},{5,4},{6,5},{7,6},{8,7},{9,8},{10,9},{11,1... | collective-permute-start | bytes 1179656 | tf_op jit(solution)/shard_map/ppermute | solution.py:17
  18.8 1.9 copy-start
  18.8 2.8 copy-start.1
  18.8 2.8 copy-start.4
  21.7 4.0 %copy-start.5 = (f32[7,8,128]{2,1,0:T(8,128)S(1)}, f32[7,8,128]{2,1,0:T(8,128)}, u32[]{:S(2)}) copy-start(f32[7,8,128]{2,1,0:T(8,128)} %param.15) | copy-start | bytes 86020
  26.1 0.7 copy-start.3
  26.1 0.7 copy-start.10
  26.8 34.4 %copy-start.8 = (pred[4096]{0:T(1024)(128)(4,1)S(1)}, pred[4096]{0:T(1024)(128)(4,1)}, u32[]{:S(2)}) copy-start(pred[4096]{0:T(1024)(128)(4,1)} %get-tuple-element.61) | copy-start | bytes 12292
  26.8 34.4 %copy-start.9 = (pred[4096]{0:T(1024)(128)(4,1)S(1)}, pred[4096]{0:T(1024)(128)(4,1)}, u32[]{:S(2)}) copy-start(pred[4096]{0:T(1024)(128)(4,1)} %get-tuple-element.62) | copy-start | bytes 12292
  130.8 31.3 %all-to-all-start.2 = ((f32[4,2,4096]{2,1,0:T(2,128)}), f32[4,2,4096]{2,1,0:T(2,128)S(1)}, u32[]{:S(2)}, u32[]{:S(2)}) async-start(f32[4,2,4096]{2,1,0:T(2,128)} %broadcast_in_dim.73), calls=%async_computation.2 | async-start | bytes 262144 | tf_op jit(solution)/shard_map/all_to_all | solution.py:24
  162.0 5.7 %copy-start.6 = (f32[4096]{0:T(1024)S(1)}, f32[4096]{0:T(1024)}, u32[]{:S(2)}) copy-start(f32[4096]{0:T(1024)} %param.23) | copy-start | bytes 49156
  162.0 5.7 %copy-start.7 = (s32[4096]{0:T(1024)S(1)}, s32[4096]{0:T(1024)}, u32[]{:S(2)}) copy-start(s32[4096]{0:T(1024)} %param.20) | copy-start | bytes 49156
  162.0 76.0 %all-to-all-start = ((f32[4,1,196608]{2,1,0:T(1,128)}), f32[4,1,196608]{2,1,0:T(1,128)S(1)}, u32[]{:S(2)}, u32[]{:S(2)}) async-start(f32[4,1,196608]{2,1,0:T(1,128)} %reshape.125), calls=%async_computation | async-start | bytes 6291456 | tf_op jit(solution)/shard_map/all_to_all | solution.py:137
  167.8 0.7 copy-start.2
where the time goes:
time: 362 us; the launch traced here: 355 us
  blocking collectives  130 us (36%)
  local copies, waits for them, and re-layouts  79.8 us (22%)
  waiting for transfers between devices  61.9 us (17%)
  starting transfers between devices  29.4 us (8%)
  other arithmetic  29.2 us (8%)
  matrix products  22 us (6%)
    all_to_all x1, blocking collectives, on_device(): lax.all_to_all(updated, 'member', split_axis=0, concat_axis=3, tiled=True)  72.7 us
    all_to_all x1, waiting for transfers between devices, on_device(): lax.all_to_all(flattened, 'member', split_axis=3, concat_axis=0, tiled=True)  61.8 us
    all_to_all x1, blocking collectives, copy_for_each(): lax.all_to_all(jnp.broadcast_to(value[None], (count, *value.shape)), axis...  57.5 us
    unnamed x25, local copies, waits for them, and re-layouts  25 us
    dot_general x4, matrix products, sunlit_update(): jnp.einsum('ji,mi...->mj...', interaction, column_block, precision=lax.Pr...  16.1 us
    all_to_all x1, starting transfers between devices, copy_for_each(): lax.all_to_all(jnp.broadcast_to(value[None], (count, *value.shape)), axis...  16 us
    all_to_all x4, local copies, waits for them, and re-layouts, on_device(): lax.all_to_all(flattened, 'member', split_axis=3, concat_axis=0, tiled=True)  15.5 us
    gather x1, local copies, waits for them, and re-layouts, on_device(): picked = jnp.take(surface, jnp.clip(local_cell, 0, cells_tile - 1), axis=1)  15.2 us
  transfers between devices with their start and end apart: 4, of which 1 were waited for; matrix products, arithmetic and copies ran while one was open for 9% of the time, Pallas kernels for 0%

commit v1 on v0

v1 whole, which is shorter than its diff:
```python
import functools

import jax
import jax.numpy as jnp
from jax import lax
from jax.experimental import pallas as pl
from jax.experimental.pallas import tpu as pltpu
from jax.sharding import PartitionSpec as P

NSUB = 4
GROUP = 8
DEEP = 2
QROWS = 2
OBS_STEP = 512
F32 = jnp.float32
MESH = pl.DeviceIdType.MESH
HIGHEST = lax.Precision.HIGHEST


def split_coefficients(interaction):
    high = lax.reduce_precision(interaction, 8, 7)
    low = interaction - high
    return jnp.concatenate([high, high, low], axis=1).astype(jnp.bfloat16)


def kernel(
    sizes,
    sunlit,
    tracers,
    horiz_mix,
    vert_mix,
    coefficients,
    remin,
    obs_cell,
    obs_tile,
    obs_value,
    obs_noise,
    obs_var,
    out,
    raw,
    mixed,
    states,
    results,
    passed,
    surface,
    partial,
    recv_mid,
    held_mid,
    recv_deep,
    held_group,
    recv_group,
    splats,
    load_sem,
    halo_send,
    halo_recv,
    state_send,
    state_recv,
    result_send,
    result_recv,
    store_sem,
    mid_send,
    mid_recv,
    deep_send,
    deep_recv,
    group_send,
    group_recv,
):
    tiles, mids, deeps = sizes
    ntr, levels, rows, cols = tracers.shape[1:]
    pair, quarters = 2, rows // QROWS
    members = 8
    pieces = levels * quarters
    me = lax.axis_index("member")
    tile = lax.axis_index("space")
    inner = (me == 1) | (me == 2)
    outer = jnp.logical_not(inner)
    group_at = lax.rem(tile, GROUP)
    mid_at = lax.rem(tile // GROUP, mids)
    deep_at = tile // (GROUP * mids)
    near = jnp.where(me == 0, 1, 2)
    beside = jnp.where(me == 1, 0, 3)
    across = jnp.where(inner, 3 - me, jnp.where(me == 0, 2, 1))

    def mid_tile(j):
        return (deep_at * mids + lax.rem(mid_at + j, mids)) * GROUP + group_at

    def deep_tile(j):
        return (lax.rem(deep_at + j, deeps) * mids + mid_at) * GROUP + group_at

    def group_tile(j):
        return (deep_at * mids + mid_at) * GROUP + lax.rem(group_at + j, GROUP)

    def load(level, row, m):
        return pltpu.make_async_copy(
            tracers.at[m, :, level, row], raw.at[level, row + 1, m], load_sem.at[level, row, m]
        )

    def start_level(level, carry):
        for row in (0, rows - 1, *range(1, rows - 1)):
            for m in range(pair):
                load(level, row, m).start()
        return carry

    lax.fori_loop(0, levels, start_level, 0)

    barrier = pltpu.get_barrier_semaphore()
    for j in range(1, 4):
        pl.semaphore_signal(
            barrier, 1, device_id=(lax.rem(me + j, 4), tile), device_id_type=MESH
        )

    @pl.when(tile > 0)
    def _():
        pl.semaphore_signal(barrier, 1, device_id=(me, tile - 1), device_id_type=MESH)

    @pl.when(tile < tiles - 1)
    def _():
        pl.semaphore_signal(barrier, 1, device_id=(me, tile + 1), device_id_type=MESH)

    @pl.when(inner)
    def _():
        for j in range(1, mids):
            pl.semaphore_signal(barrier, 1, device_id=(me, mid_tile(j)), device_id_type=MESH)
        for j in range(1, deeps):
            pl.semaphore_signal(barrier, 1, device_id=(me, deep_tile(j)), device_id_type=MESH)
        for j in range(1, GROUP):
            pl.semaphore_signal(barrier, 1, device_id=(me, group_tile(j)), device_id_type=MESH)

    peers = 3 + (tile > 0).astype(jnp.int32) + (tile < tiles - 1).astype(jnp.int32)
    peers += jnp.where(inner, mids + deeps + GROUP - 3, 0)
    pl.semaphore_wait(barrier, peers)

    def halo_up(level):
        return pltpu.make_async_remote_copy(
            src_ref=raw.at[level, rows],
            dst_ref=raw.at[level, 0],
            send_sem=halo_send.at[level, 0],
            recv_sem=halo_recv.at[level, 0],
            device_id=(me, lax.rem(tile + 1, tiles)),
            device_id_type=MESH,
        )

    def halo_down(level):
        return pltpu.make_async_remote_copy(
            src_ref=raw.at[level, 1],
            dst_ref=raw.at[level, rows + 1],
            send_sem=halo_send.at[level, 1],
            recv_sem=halo_recv.at[level, 1],
            device_id=(me, lax.rem(tile + tiles - 1, tiles)),
            device_id_type=MESH,
        )

    def send_edges(level, carry):
        for row in (0, rows - 1):
            for m in range(pair):
                load(level, row, m).wait()

        @pl.when(tile < tiles - 1)
        def _():
            halo_up(level).start()

        @pl.when(tile > 0)
        def _():
            halo_down(level).start()

        return carry

    lax.fori_loop(0, levels, send_edges, 0)

    lane = lax.broadcasted_iota(jnp.int32, (ntr, cols), 1)

    def mix_level(level):
        for row in range(1, rows - 1):
            for m in range(pair):
                load(level, row, m).wait()

        @pl.when(tile > 0)
        def _():
            halo_up(level).wait_recv()

        @pl.when(tile == 0)
        def _():
            raw[level, 0] = raw[level, 1]

        @pl.when(tile < tiles - 1)
        def _():
            halo_down(level).wait_recv()

        @pl.when(tile == tiles - 1)
        def _():
            raw[level, rows + 1] = raw[level, rows]

        def mix_row(row, carry):
            strength = horiz_mix[level, pl.ds(row, 1), :]
            for m in range(pair):
                own = raw[level, row + 1, m]
                west = jnp.where(lane == 0, own, pltpu.roll(own, 1, 1))
                east = jnp.where(lane == cols - 1, own, pltpu.roll(own, cols - 1, 1))
                laplace = raw[level, row, m] + raw[level, row + 2, m] + west + east - 4.0 * own
                mixed[level, row, m] = own + strength * laplace
            return carry

        lax.fori_loop(0, rows, mix_row, 0)

    def state_copy(piece, to, which):
        level, quarter = piece // quarters, lax.rem(piece, quarters)
        block = states.at[level, quarter, pl.ds(2 * me, 2)]
        return pltpu.make_async_remote_copy(
            src_ref=block,
            dst_ref=block,
            send_sem=state_send.at[piece, which],
            recv_sem=state_recv.at[piece, me],
            device_id=(to, tile),
            device_id_type=MESH,
        )

    loss = jnp.broadcast_to(remin[...], (ntr, cols))
    loss = jnp.concatenate([loss] * (QROWS * pair), axis=1)
    taken = coefficients[...]

    def grow_piece(piece, carry):
        level, quarter = piece // quarters, lax.rem(piece, quarters)
        below, above = jnp.minimum(level + 1, levels - 1), jnp.maximum(level - 1, 0)
        light = 0.6 * jnp.exp(-0.4 * jnp.full((1, cols), level, jnp.int32).astype(F32))
        blocks, lights = [], []
        for r in range(QROWS):
            row = quarter * QROWS + r
            lit = (sunlit[tile * rows + row] > 0).astype(F32)
            down_mix = vert_mix[jnp.minimum(level, levels - 2), pl.ds(row, 1), :]
            up_mix = vert_mix[above, pl.ds(row, 1), :]
            for m in range(pair):
                here = mixed[level, row, m]
                down = down_mix * (mixed[below, row, m] - here)
                up = up_mix * (here - mixed[above, row, m])
                blocks.append(here + down - up)
                lights.append(light * lit)
        value = jnp.concatenate(blocks, axis=1)
        light = jnp.concatenate(lights, axis=1)
        for _ in range(NSUB):
            high = value.astype(jnp.bfloat16)
            low = (value - high.astype(F32)).astype(jnp.bfloat16)
            uptake = jnp.dot(
                taken, jnp.concatenate([high, low, high], axis=0), preferred_element_type=F32
            )
            value = value + (1.0 / NSUB) * (light * jnp.tanh(uptake) - loss * value)
        for r in range(QROWS):
            for m in range(pair):
                at = (r * pair + m) * cols
                states[level, quarter, 2 * me + m, r] = value[:, at : at + cols]
        state_copy(piece, across, 0).start()

        @pl.when(outer)
        def _():
            state_copy(piece, near, 1).start()

        return carry

    mix_level(0)

    def step_level(level, carry):
        @pl.when(level < levels - 1)
        def _():
            mix_level(level + 1)

        return lax.fori_loop(level * quarters, (level + 1) * quarters, grow_piece, carry)

    lax.fori_loop(0, levels, step_level, 0)

    def wait_states(piece):
        level, quarter = piece // quarters, lax.rem(piece, quarters)
        for j in range(1, 4):
            source = lax.rem(me + j, 4)
            block = states.at[level, quarter, pl.ds(2 * source, 2)]
            pltpu.make_async_remote_copy(
                src_ref=block,
                dst_ref=block,
                send_sem=state_send.at[piece, 0],
                recv_sem=state_recv.at[piece, source],
                device_id=(source, tile),
                device_id_type=MESH,
            ).wait_recv()

    def result_copy(piece):
        return pltpu.make_async_remote_copy(
            src_ref=passed.at[piece],
            dst_ref=results.at[piece],
            send_sem=result_send.at[piece],
            recv_sem=result_recv.at[piece],
            device_id=(beside, tile),
            device_id_type=MESH,
        )

    def stores(piece):
        level, quarter = piece // quarters, lax.rem(piece, quarters)
        return [
            pltpu.make_async_copy(
                results.at[piece, m, r],
                out.at[m, :, level, quarter * QROWS + r],
                store_sem.at[piece, m, r],
            )
            for m in range(pair)
            for r in range(QROWS)
        ]

    def small_copy(source, target, send, recv, at):
        return pltpu.make_async_remote_copy(
            src_ref=source,
            dst_ref=target,
            send_sem=send,
            recv_sem=recv,
            device_id=(me, at),
            device_id_type=MESH,
        )

    def partial_sums():
        for quarter in range(quarters):
            for r in range(QROWS):
                for m in range(members):
                    at = (quarter * QROWS + r) * members + m
                    surface[at : at + 1, :] = states[0, quarter, m, r, 0:1, :]
        picked_from = surface[...]
        width = OBS_STEP // cols
        column_ids = lax.broadcasted_iota(jnp.int32, (cols, OBS_STEP), 0)
        tile_ids = lax.broadcasted_iota(jnp.int32, (tiles, OBS_STEP), 0)

        def flat(ref, step):
            return jnp.concatenate(
                [ref[pl.ds(step * width + i, 1), :] for i in range(width)], axis=1
            )

        def step_obs(step, total):
            local = flat(obs_cell, step) - tile * (rows * cols)
            column = jnp.bitwise_and(local, cols - 1)
            row_of = jnp.right_shift(local, cols.bit_length() - 1)
            one_hot = (column_ids == column).astype(F32)
            picked = jnp.dot(
                picked_from, one_hot, precision=HIGHEST, preferred_element_type=F32
            )
            observed = jnp.zeros((members, OBS_STEP), F32)
            for r in range(rows):
                observed += jnp.where(
                    row_of == r, picked[r * members : (r + 1) * members], 0.0
                )
            inside = (row_of >= 0) & (row_of < rows)
            weight = jnp.where(inside, 1.0 / flat(obs_var, step), 0.0)
            spread = observed - jnp.sum(observed, axis=0, keepdims=True) * (1.0 / members)
            noise = obs_noise[:, pl.ds(pl.multiple_of(step * OBS_STEP, OBS_STEP), OBS_STEP)]
            innov = flat(obs_value, step) + noise - observed
            scaled = spread * weight
            both = jnp.concatenate([spread, innov], axis=0)
            products = jnp.concatenate(
                [scaled[a : a + 1] * both for a in range(members)], axis=0
            )
            chosen = (tile_ids == flat(obs_tile, step)).astype(F32)
            return total + lax.dot_general(
                chosen,
                products,
                (((1,), (1,)), ((), ())),
                precision=HIGHEST,
                preferred_element_type=F32,
            )

        steps = obs_noise.shape[1] // OBS_STEP
        total = lax.fori_loop(0, steps, step_obs, jnp.zeros((tiles, 128), F32))
        for d in range(deeps):
            for b in range(mids):
                at = (d * mids + b) * GROUP
                partial[b, d] = total[at : at + GROUP]

        copies = []
        for j in range(1, mids):
            other = lax.rem(mid_at + j, mids)
            copies.append(
                small_copy(
                    partial.at[other],
                    recv_mid.at[mid_at],
                    mid_send.at[j],
                    mid_recv.at[mid_at],
                    mid_tile(j),
                )
            )
        for copy in copies:
            copy.start()
        sums = partial[mid_at]
        for j in range(1, mids):
            other = lax.rem(mid_at + j, mids)
            small_copy(
                recv_mid.at[other],
                recv_mid.at[other],
                mid_send.at[j],
                mid_recv.at[other],
                mid_tile(j),
            ).wait_recv()
            sums = sums + recv_mid[other]
        held_mid[...] = sums
        for j in range(1, deeps):
            other = lax.rem(deep_at + j, deeps)
            copies.append(
                small_copy(
                    held_mid.at[other],
                    recv_deep.at[deep_at],
                    deep_send.at[j],
                    deep_recv.at[deep_at],
                    deep_tile(j),
                )
            )
            copies[-1].start()
        sums = held_mid[deep_at]
        for j in range(1, deeps):
            other = lax.rem(deep_at + j, deeps)
            small_copy(
                recv_deep.at[other],
                recv_deep.at[other],
                deep_send.at[j],
                deep_recv.at[other],
                deep_tile(j),
            ).wait_recv()
            sums = sums + recv_deep[other]
        held_group[...] = sums
        for j in range(1, GROUP):
            copies.append(
                small_copy(
                    held_group,
                    recv_group.at[group_at],
                    group_send.at[j],
                    group_recv.at[group_at],
                    group_tile(j),
                )
            )
            copies[-1].start()
        for j in range(1, GROUP):
            other = lax.rem(group_at + j, GROUP)
            small_copy(
                held_group,
                recv_group.at[other],
                group_send.at[j],
                group_recv.at[other],
                group_tile(j),
            ).wait_recv()
            sums = sums + recv_group[other]
        for copy in copies:
            copy.wait_send()
        return sums

    def weights_of(sums):
        sub = lax.broadcasted_iota(jnp.int32, (8, 128), 0)
        lane8 = lax.broadcasted_iota(jnp.int32, (8, 128), 1)
        own = jnp.sum(jnp.where(sub == group_at, sums, 0.0), axis=0, keepdims=True)
        parts = jnp.where(
            jnp.right_shift(lane8, 4) == sub, jnp.broadcast_to(own, (8, 128)), 0.0
        )
        fold_from = lax.broadcasted_iota(jnp.int32, (128, 128), 0)
        fold_to = lax.broadcasted_iota(jnp.int32, (128, 128), 1)
        fold = (jnp.bitwise_and(fold_from, 15) == fold_to).astype(F32)
        system = jnp.dot(parts, fold, precision=HIGHEST, preferred_element_type=F32)
        system = system + jnp.where(lane8 == sub, float(members - 1), 0.0)
        for k in range(members):
            column = jnp.sum(jnp.where(lane8 == k, system, 0.0), axis=1, keepdims=True)
            pivot = system[k : k + 1] / column[k : k + 1]
            system = jnp.where(sub == k, pivot, system - column * pivot)
        return system - jnp.sum(system, axis=0, keepdims=True) * (1.0 / members)

    def spread_weights(centered):
        sub = lax.broadcasted_iota(jnp.int32, (8, 128), 0)
        lane8 = lax.broadcasted_iota(jnp.int32, (8, 128), 1)
        for j in range(4):
            member = 2 * me + j if j < 2 else 2 * beside + j - 2
            column = jnp.sum(
                jnp.where(lane8 == members + member, centered, 0.0), axis=1, keepdims=True
            )
            wide = jnp.broadcast_to(column, (8, 128))
            wide = wide + jnp.where(sub == member, 1.0, 0.0)
            for k in range(members):
                splats[j, k] = jnp.broadcast_to(wide[k : k + 1], (8, 128))

    def analyse(piece):
        level, quarter = piece // quarters, lax.rem(piece, quarters)

        def analyse_part(at, carry):
            r, first = at // (ntr // 8), pl.multiple_of(lax.rem(at, ntr // 8) * 8, 8)
            sums = [None] * 4
            for k in range(members):
                value = states[level, quarter, k, r, pl.ds(first, 8), :]
                for j in range(4):
                    term = value * splats[j, k]
                    sums[j] = term if k == 0 else sums[j] + term
            for m in range(pair):
                results[piece, m, r, pl.ds(first, 8), :] = sums[m]
                passed[piece, m, r, pl.ds(first, 8), :] = sums[2 + m]
            return carry

        lax.fori_loop(0, QROWS * (ntr // 8), analyse_part, 0)
        result_copy(piece).start()
        for store in stores(piece):
            store.start()

    @pl.when(inner)
    def _():
        def wait_top(piece, carry):
            wait_states(piece)
            return carry

        lax.fori_loop(0, quarters, wait_top, 0)
        spread_weights(weights_of(partial_sums()))

        def analyse_top(piece, carry):
            analyse(piece)
            return carry

        def analyse_next(piece, carry):
            wait_states(piece)
            analyse(piece)
            return carry

        lax.fori_loop(0, quarters, analyse_top, 0)
        lax.fori_loop(quarters, pieces, analyse_next, 0)

    @pl.when(outer)
    def _():
        def take(piece, carry):
            result_copy(piece).wait_recv()
            for store in stores(piece):
                store.start()
            return carry

        lax.fori_loop(0, pieces, take, 0)

    def finish_level(level, carry):
        @pl.when(tile < tiles - 1)
        def _():
            halo_up(level).wait_send()

        @pl.when(tile > 0)
        def _():
            halo_down(level).wait_send()

        return carry

    lax.fori_loop(0, levels, finish_level, 0)

    def finish(piece, carry):
        state_copy(piece, across, 0).wait_send()

        @pl.when(outer)
        def _():
            state_copy(piece, near, 1).wait_send()

        @pl.when(inner)
        def _():
            result_copy(piece).wait_send()

        for store in stores(piece):
            store.wait()
        return carry

    lax.fori_loop(0, pieces, finish, 0)


def on_device(
    tracers,
    horiz_mix,
    vert_mix,
    sunlit,
    interaction,
    remin,
    obs_cell,
    obs_tile,
    obs_value,
    obs_noise,
    obs_var,
):
    pair, ntr, levels, rows, cols = tracers.shape
    tiles = lax.axis_size("space")
    deeps = DEEP if tiles > GROUP else 1
    mids = tiles // (deeps * GROUP)
    quarters = rows // QROWS
    pieces = levels * quarters
    count = obs_cell.shape[0]
    obs_rows = (count // cols, cols)
    vmem = pl.BlockSpec(memory_space=pltpu.VMEM)
    anywhere = pl.BlockSpec(memory_space=pl.ANY)
    dma = pltpu.SemaphoreType.DMA
    result = pl.pallas_call(
        functools.partial(kernel, (tiles, mids, deeps)),
        out_shape=jax.ShapeDtypeStruct(tracers.shape, F32),
        in_specs=[pl.BlockSpec(memory_space=pltpu.SMEM), anywhere] + [vmem] * 9,
        out_specs=anywhere,
        scratch_shapes=[
            pltpu.VMEM((levels, rows + 2, pair, ntr, cols), F32),
            pltpu.VMEM((levels, rows, pair, ntr, cols), F32),
            pltpu.VMEM((levels, quarters, 8, QROWS, ntr, cols), F32),
            pltpu.VMEM((pieces, pair, QROWS, ntr, cols), F32),
            pltpu.VMEM((pieces, pair, QROWS, ntr, cols), F32),
            pltpu.VMEM((rows * 8, cols), F32),
            pltpu.VMEM((mids, deeps, GROUP, 128), F32),
            pltpu.VMEM((mids, deeps, GROUP, 128), F32),
            pltpu.VMEM((deeps, GROUP, 128), F32),
            pltpu.VMEM((deeps, GROUP, 128), F32),
            pltpu.VMEM((GROUP, 128), F32),
            pltpu.VMEM((GROUP, GROUP, 128), F32),
            pltpu.VMEM((4, 8, 8, 128), F32),
            dma((levels, rows, pair)),
            dma((levels, 2)),
            dma((levels, 2)),
            dma((pieces, 2)),
            dma((pieces, 4)),
            dma((pieces,)),
            dma((pieces,)),
            dma((pieces, pair, QROWS)),
            dma((mids,)),
            dma((mids,)),
            dma((deeps,)),
            dma((deeps,)),
            dma((GROUP,)),
            dma((GROUP,)),
        ],
        compiler_params=pltpu.CompilerParams(
            collective_id=0, has_side_effects=True, vmem_limit_bytes=56 * 1024 * 1024
        ),
        cost_estimate=pl.CostEstimate(
            flops=500_000_000, bytes_accessed=8_000_000, transcendentals=3_000_000
        ),
        name="step_and_analysis",
    )(
        sunlit,
        tracers,
        horiz_mix,
        vert_mix,
        split_coefficients(interaction),
        remin.reshape(ntr, 1),
        obs_cell.reshape(obs_rows),
        obs_tile.reshape(obs_rows),
        obs_value.reshape(obs_rows),
        obs_noise,
        obs_var.reshape(obs_rows),
    )
    return result


def solution(mesh):
    return jax.shard_map(
        on_device,
        mesh=mesh,
        in_specs=(
            P("member", None, None, "space", None),
            P(None, "space", None),
            P(None, "space", None),
            P(),
            P(),
            P(),
            P(),
            P(),
            P(),
            P(),
            P(),
        ),
        out_specs=P("member", None, None, "space", None),
        check_vma=False,
    )
```

time: 362 us -> 169 us (0.47)
  the two profiles are of different devices: /device:TPU:8 before, /device:TPU:224 now
where the time goes in v1:
time: 169 us; the launch traced here: 166 us
  Pallas kernels  160 us (95%)
  local copies, waits for them, and re-layouts  5.31 us (3%)
    pallas_call x1, Pallas kernels, on_device(): pl.pallas_call(functools.partial(kernel, (tiles, mids, deeps)), out_shape...  160 us
    unnamed x1, local copies, waits for them, and re-layouts  3.97 us

profile of v1, /device:TPU:224, one launch (start us, length us, event | category | flops | bytes accessed | tf_op | source)
XLA Modules:
  0.0 166.4 jit_solution(8137024508598652865)
XLA Ops:
  0.0 1.3 copy.12.remin
  1.3 0.7 reduce-precision_convert_fusion
  2.1 0.7 pad_maximum_fusion.coefficients
  2.8 159.7 %step_and_analysis.1 = f32[2,48,8,8,128]{4,3,2,1,0:T(8,128)} custom-call(s32[512]{0:T(512)} %sunlit.1, f32[2,48,8,8,128]{4,3,2,1,0:T(8,128)} %tracers.1, f32[8,8,128]{2,1,0:T(8,128)} %horiz_mix.1, f32[7,8,128]{2,1,0:T(8,128)} %vert_mix.1, bf16[48,144]{1,0:T(8,128)(2,1)} %pad_maximum_fusion.coefficients, f32[48,1]{1,0:T(8,128)} %copy.12.remin, ...), custom_call_target="tpu_custom_call" | custom-call | flops 500000000 | bytes 8000000 | tf_op jit(solution)/shard_map/step_and_analysis/pallas_call | solution.py:583
  162.5 4.0 %copy.14 = f32[2,48,8,8,128]{4,3,2,1,0:T(8,128)} copy(f32[2,48,8,8,128]{4,3,2,1,0:T(8,128)} %step_and_analysis.1) | data formatting | bytes 6291456

commit v2 on v1

--- a/solution.py
+++ b/solution.py
@@ -11,32 +11,40 @@
 GROUP = 8
 DEEP = 2
 QROWS = 2
+LAG = 2
+VMEM_BYTES = 34 * 1024 * 1024
 OBS_STEP = 512
 F32 = jnp.float32
 MESH = pl.DeviceIdType.MESH
 HIGHEST = lax.Precision.HIGHEST
 
 
-def split_coefficients(interaction):
-    high = lax.reduce_precision(interaction, 8, 7)
-    low = interaction - high
-    return jnp.concatenate([high, high, low], axis=1).astype(jnp.bfloat16)
-
-
 def kernel(
     sizes,
-    sunlit,
     tracers,
+    horiz_from,
+    vert_from,
+    sunlit_from,
+    interaction_from,
+    remin_from,
+    cell_from,
+    chosen_from,
+    value_from,
+    noise_from,
+    var_from,
+    out,
     horiz_mix,
     vert_mix,
-    coefficients,
+    sunlit,
+    interaction,
     remin,
     obs_cell,
     obs_tile,
     obs_value,
     obs_noise,
     obs_var,
-    out,
+    lit,
+    relayed,
     raw,
     mixed,
     states,
@@ -50,7 +58,10 @@
     held_group,
     recv_group,
     splats,
+    small_sem,
     load_sem,
+    relay_send,
+    relay_recv,
     halo_send,
     halo_recv,
     state_send,
@@ -77,6 +88,16 @@
     group_at = lax.rem(tile, GROUP)
     mid_at = lax.rem(tile // GROUP, mids)
     deep_at = tile // (GROUP * mids)
+    half = tiles // 2
+    is_up_relay = (tile < half) & (lax.rem(tile, 4) == 2)
+    is_down_relay = (tile >= half) & (lax.rem(tile, 4) == 1)
+
+    def up_relay(level):
+        return 4 * level + 2
+
+    def down_relay(level):
+        return half + 4 * level + 1
+
     near = jnp.where(me == 0, 1, 2)
     beside = jnp.where(me == 1, 0, 3)
     across = jnp.where(inner, 3 - me, jnp.where(me == 0, 2, 1))
@@ -90,18 +111,10 @@
     def group_tile(j):
         return (deep_at * mids + mid_at) * GROUP + lax.rem(group_at + j, GROUP)
 
-    def load(level, row, m):
+    def load(level, row):
         return pltpu.make_async_copy(
-            tracers.at[m, :, level, row], raw.at[level, row + 1, m], load_sem.at[level, row, m]
-        )
-
-    def start_level(level, carry):
-        for row in (0, rows - 1, *range(1, rows - 1)):
-            for m in range(pair):
-                load(level, row, m).start()
-        return carry
-
-    lax.fori_loop(0, levels, start_level, 0)
+            tracers.at[:, :, level, row], raw.at[level, row + 1], load_sem.at[level, row]
+        )
 
     barrier = pltpu.get_barrier_semaphore()
     for j in range(1, 4):
@@ -126,9 +139,59 @@
         for j in range(1, GROUP):
             pl.semaphore_signal(barrier, 1, device_id=(me, group_tile(j)), device_id_type=MESH)
 
-    peers = 3 + (tile > 0).astype(jnp.int32) + (tile < tiles - 1).astype(jnp.int32)
-    peers += jnp.where(inner, mids + deeps + GROUP - 3, 0)
-    pl.semaphore_wait(barrier, peers)
+    if deeps > 1:
+
+        @pl.when(tile == half - 1)
+        def _():
+            for level in range(levels):
+                pl.semaphore_signal(
+                    barrier, 1, device_id=(me, down_relay(level)), device_id_type=MESH
+                )
+
+        @pl.when(tile == half)
+        def _():
+            for level in range(levels):
+                pl.semaphore_signal(
+                    barrier, 1, device_id=(me, up_relay(level)), device_id_type=MESH
+                )
+
+        @pl.when(is_up_relay)
+        def _():
+            pl.semaphore_signal(barrier, 1, device_id=(me, half - 1), device_id_type=MESH)
+
+        @pl.when(is_down_relay)
+        def _():
+            pl.semaphore_signal(barrier, 1, device_id=(me, half), device_id_type=MESH)
+
+    def small(at):
+        source, held = (
+            (interaction_from, interaction),
+            (remin_from, remin),
+            (sunlit_from, sunlit),
+            (horiz_from, horiz_mix),
+            (vert_from, vert_mix),
+            (cell_from, obs_cell),
+            (chosen_from, obs_tile),
+            (value_from, obs_value),
+            (noise_from, obs_noise),
+            (var_from, obs_var),
+        )[at]
+        return pltpu.make_async_copy(source, held, small_sem.at[at])
+
+    for at in range(5):
+        small(at).start()
+
+    def start_middle(level, carry):
+        for row in range(1, rows - 1):
+            load(level, row).start()
+        return carry
+
+    def start_edges(level, carry):
+        for row in (0, rows - 1):
+            load(level, row).start()
+        return carry
+
+    lax.fori_loop(0, 2, start_middle, 0)
 
     def halo_up(level):
         return pltpu.make_async_remote_copy(
@@ -150,57 +213,116 @@
             device_id_type=MESH,
         )
 
+    def to_relay(level, row, way, at):
+        return pltpu.make_async_remote_copy(
+            src_ref=raw.at[level, row],
+            dst_ref=relayed,
+            send_sem=halo_send.at[level, way],
+            recv_sem=relay_recv,
+            device_id=(me, at),
+            device_id_type=MESH,
+        )
+
+    def from_relay(level, row, way, at):
+        return pltpu.make_async_remote_copy(
+            src_ref=relayed,
+            dst_ref=raw.at[level, row],
+            send_sem=relay_send,
+            recv_sem=halo_recv.at[level, way],
+            device_id=(me, at),
+            device_id_type=MESH,
+        )
+
+    def pass_on():
+        @pl.when(is_up_relay)
+        def _():
+            level = tile // 4
+            to_relay(level, rows, 0, half - 1).wait_recv()
+            from_relay(level, 0, 0, half).start()
+
+        @pl.when(is_down_relay)
+        def _():
+            level = (tile - half) // 4
+            to_relay(level, 1, 1, half).wait_recv()
+            from_relay(level, rows + 1, 1, half - 1).start()
+
+    def end_pass():
+        @pl.when(is_up_relay)
+        def _():
+            from_relay(tile // 4, 0, 0, half).wait_send()
+
+        @pl.when(is_down_relay)
+        def _():
+            from_relay((tile - half) // 4, rows + 1, 1, half - 1).wait_send()
+
     def send_edges(level, carry):
         for row in (0, rows - 1):
-            for m in range(pair):
-                load(level, row, m).wait()
+            load(level, row).wait()
+
+        @pl.when((tile < tiles - 1) & (tile != half - 1))
+        def _():
+            halo_up(level).start()
+
+        @pl.when((tile > 0) & (tile != half))
+        def _():
+            halo_down(level).start()
+
+        if deeps > 1:
+
+            @pl.when(tile == half - 1)
+            def _():
+                to_relay(level, rows, 0, up_relay(level)).start()
+
+            @pl.when(tile == half)
+            def _():
+                to_relay(level, 1, 1, down_relay(level)).start()
+
+        return carry
+
+    lane = lax.broadcasted_iota(jnp.int32, (ntr, cols), 1)
+
+    def mix_row(level, row):
+        strength = horiz_mix[level, pl.ds(row, 1), :]
+        for m in range(pair):
+            own = raw[level, row + 1, m]
+            west = jnp.where(lane == 0, own, pltpu.roll(own, 1, 1))
+            east = jnp.where(lane == cols - 1, own, pltpu.roll(own, cols - 1, 1))
+            laplace = raw[level, row, m] + raw[level, row + 2, m] + west + east - 4.0 * own
+            mixed[level, row, m] = own + strength * laplace
+
+    def mix_middle(level):
+        for row in range(1, rows - 1):
+            load(level, row).wait()
+
+        def mix_one(row, carry):
+            mix_row(level, row)
+            return carry
+
+        lax.fori_loop(QROWS, rows - QROWS, mix_one, 0)
+
+    def mix_edges(level):
+        @pl.when(tile > 0)
+        def _():
+            halo_up(level).wait_recv()
+
+        @pl.when(tile == 0)
+        def _():
+            raw[level, 0] = raw[level, 1]
 
         @pl.when(tile < tiles - 1)
         def _():
-            halo_up(level).start()
-
-        @pl.when(tile > 0)
-        def _():
-            halo_down(level).start()
-
-        return carry
-
-    lax.fori_loop(0, levels, send_edges, 0)
-
-    lane = lax.broadcasted_iota(jnp.int32, (ntr, cols), 1)
-
-    def mix_level(level):
-        for row in range(1, rows - 1):
-            for m in range(pair):
-                load(level, row, m).wait()
-
-        @pl.when(tile > 0)
-        def _():
-            halo_up(level).wait_recv()
-
-        @pl.when(tile == 0)
-        def _():
-            raw[level, 0] = raw[level, 1]
-
-        @pl.when(tile < tiles - 1)
-        def _():
             halo_down(level).wait_recv()
 
         @pl.when(tile == tiles - 1)
         def _():
             raw[level, rows + 1] = raw[level, rows]
 
-        def mix_row(row, carry):
-            strength = horiz_mix[level, pl.ds(row, 1), :]
-            for m in range(pair):
-                own = raw[level, row + 1, m]
-                west = jnp.where(lane == 0, own, pltpu.roll(own, 1, 1))
-                east = jnp.where(lane == cols - 1, own, pltpu.roll(own, cols - 1, 1))
-                laplace = raw[level, row, m] + raw[level, row + 2, m] + west + east - 4.0 * own
-                mixed[level, row, m] = own + strength * laplace
+        def mix_two(row, carry):
+            mix_row(level, row)
+            mix_row(level, rows - 1 - row)
             return carry
 
-        lax.fori_loop(0, rows, mix_row, 0)
+        lax.fori_loop(0, QROWS, mix_two, 0)
 
     def state_copy(piece, to, which):
         level, quarter = piece // quarters, lax.rem(piece, quarters)
@@ -214,18 +336,37 @@
             device_id_type=MESH,
         )
 
-    loss = jnp.broadcast_to(remin[...], (ntr, cols))
+    for at in range(5):
+        small(at).wait()
+    same = lax.broadcasted_iota(jnp.int32, (ntr, ntr), 0) == lax.broadcasted_iota(
+        jnp.int32, (ntr, ntr), 1
+    )
+    loss = jnp.sum(
+        jnp.where(same, jnp.broadcast_to(remin[...], (ntr, ntr)), 0.0), axis=1, keepdims=True
+    )
+    loss = jnp.broadcast_to(loss, (ntr, cols))
     loss = jnp.concatenate([loss] * (QROWS * pair), axis=1)
-    taken = coefficients[...]
-
-    def grow_piece(piece, carry):
-        level, quarter = piece // quarters, lax.rem(piece, quarters)
+    place_from = lax.broadcasted_iota(jnp.int32, (ntr, 3 * ntr), 0)
+    place_to = lax.broadcasted_iota(jnp.int32, (ntr, 3 * ntr), 1)
+    place = (lax.rem(place_to, ntr) == place_from).astype(F32)
+    wide = jnp.dot(interaction[...], place, precision=HIGHEST, preferred_element_type=F32)
+    wide_high = wide.astype(jnp.bfloat16).astype(F32)
+    taken = jnp.where(place_to < 2 * ntr, wide_high, wide - wide_high).astype(jnp.bfloat16)
+
+    flags = (sunlit[pl.ds(tile * rows // cols, 1), :] > 0).astype(F32)
+    flag_lane = lax.broadcasted_iota(jnp.int32, (1, cols), 1)
+    for row in range(rows):
+        flag = jnp.where(flag_lane == lax.rem(tile * rows, cols) + row, flags, 0.0)
+        lit[row : row + 1, :] = jnp.broadcast_to(
+            jnp.sum(flag, axis=1, keepdims=True), (1, cols)
+        )
+
+    def grow(level, quarter):
         below, above = jnp.minimum(level + 1, levels - 1), jnp.maximum(level - 1, 0)
         light = 0.6 * jnp.exp(-0.4 * jnp.full((1, cols), level, jnp.int32).astype(F32))
         blocks, lights = [], []
         for r in range(QROWS):
             row = quarter * QROWS + r
-            lit = (sunlit[tile * rows + row] > 0).astype(F32)
             down_mix = vert_mix[jnp.minimum(level, levels - 2), pl.ds(row, 1), :]
             up_mix = vert_mix[above, pl.ds(row, 1), :]
             for m in range(pair):
@@ -233,7 +374,7 @@
                 down = down_mix * (mixed[below, row, m] - here)
                 up = up_mix * (here - mixed[above, row, m])
                 blocks.append(here + down - up)
-                lights.append(light * lit)
+                lights.append(light * lit[pl.ds(row, 1), :])
         value = jnp.concatenate(blocks, axis=1)
         light = jnp.concatenate(lights, axis=1)
         for _ in range(NSUB):
@@ -247,24 +388,82 @@
             for m in range(pair):
                 at = (r * pair + m) * cols
                 states[level, quarter, 2 * me + m, r] = value[:, at : at + cols]
+
+    def send(level, quarter):
+        piece = level * quarters + quarter
         state_copy(piece, across, 0).start()
 
         @pl.when(outer)
         def _():
             state_copy(piece, near, 1).start()
 
-        return carry
-
-    mix_level(0)
+    lax.fori_loop(0, levels, start_edges, 0)
+    lax.fori_loop(2, levels, start_middle, 0)
+
+    @pl.when(inner)
+    def _():
+        for at in range(5, 10):
+            small(at).start()
+
+    mix_middle(0)
+    mix_middle(1)
+    grow(0, 1)
+
+    peers = 3 + (tile > 0).astype(jnp.int32) + (tile < tiles - 1).astype(jnp.int32)
+    peers += jnp.where(inner, mids + deeps + GROUP - 3, 0)
+    if deeps > 1:
+        peers += (is_up_relay | is_down_relay).astype(jnp.int32)
+        peers += jnp.where((tile == half - 1) | (tile == half), levels, 0)
+    pl.semaphore_wait(barrier, peers)
+
+    send(0, 1)
+    for quarter in range(2, quarters - 1):
+        grow(0, quarter)
+        send(0, quarter)
+    lax.fori_loop(0, levels, send_edges, 0)
+
+    if levels > 2:
+        mix_middle(2)
+
+    for quarter in range(1, quarters - 1):
+        grow(1, quarter)
+        send(1, quarter)
+    if deeps > 1:
+        pass_on()
+    mix_edges(0)
+    mix_edges(1)
+    for quarter in (0, quarters - 1):
+        grow(0, quarter)
+        send(0, quarter)
 
     def step_level(level, carry):
         @pl.when(level < levels - 1)
         def _():
-            mix_level(level + 1)
-
-        return lax.fori_loop(level * quarters, (level + 1) * quarters, grow_piece, carry)
-
-    lax.fori_loop(0, levels, step_level, 0)
+            mix_middle(level + 1)
+
+        for quarter in range(1, quarters - 1):
+            grow(level, quarter)
+            send(level, quarter)
+        mix_edges(level)
+        for quarter in (0, quarters - 1):
+            grow(level - 1, quarter)
+            send(level - 1, quarter)
+        return carry
+
+    lax.fori_loop(2, levels, step_level, 0)
+    for quarter in (0, quarters - 1):
+        grow(levels - 1, quarter)
+        send(levels - 1, quarter)
+
+    def in_order(step):
+        later = step - 2
+        level, turn = 1 + later // 4, lax.rem(later, 4)
+        piece = jnp.where(
+            turn < 2, level * quarters + 1 + turn, (level - 1) * quarters + 3 * (turn - 2)
+        )
+        piece = jnp.where(step < 2, 1 + step, piece)
+        ending = step - (pieces - 2)
+        return jnp.where(ending < 0, piece, (levels - 1) * quarters + 3 * ending)
 
     def wait_states(piece):
         level, quarter = piece // quarters, lax.rem(piece, quarters)
@@ -294,11 +493,10 @@
         level, quarter = piece // quarters, lax.rem(piece, quarters)
         return [
             pltpu.make_async_copy(
-                results.at[piece, m, r],
-                out.at[m, :, level, quarter * QROWS + r],
-                store_sem.at[piece, m, r],
-            )
-            for m in range(pair)
+                results.at[piece, r],
+                out.at[:, :, level, quarter * QROWS + r],
+                store_sem.at[piece, r],
+            )
             for r in range(QROWS)
         ]
 
@@ -485,8 +683,8 @@
                     term = value * splats[j, k]
                     sums[j] = term if k == 0 else sums[j] + term
             for m in range(pair):
-                results[piece, m, r, pl.ds(first, 8), :] = sums[m]
-                passed[piece, m, r, pl.ds(first, 8), :] = sums[2 + m]
+                results[piece, r, m, pl.ds(first, 8), :] = sums[m]
+                passed[piece, r, m, pl.ds(first, 8), :] = sums[2 + m]
             return carry
 
         lax.fori_loop(0, QROWS * (ntr // 8), analyse_part, 0)
@@ -494,66 +692,83 @@
         for store in stores(piece):
             store.start()
 
+    def settle(piece):
+        state_copy(piece, across, 0).wait_send()
+
+        @pl.when(outer)
+        def _():
+            state_copy(piece, near, 1).wait_send()
+
+        @pl.when(inner)
+        def _():
+            result_copy(piece).wait_send()
+
+        for store in stores(piece):
+            store.wait()
+
+    def finish_level(level, carry):
+        @pl.when(tile < tiles - 1)
+        def _():
+            halo_up(level).wait_send()
+
+        @pl.when(tile > 0)
+        def _():
+            halo_down(level).wait_send()
+
+        return carry
+
+    lax.fori_loop(0, levels, finish_level, 0)
+    if deeps > 1:
+        end_pass()
+
     @pl.when(inner)
     def _():
-        def wait_top(piece, carry):
-            wait_states(piece)
+        for at in range(5, 10):
+            small(at).wait()
+        for quarter in range(1, quarters - 1):
+            wait_states(quarter)
+        for quarter in (0, quarters - 1):
+            wait_states(quarter)
+        spread_weights(weights_of(partial_sums()))
+
+        def analyse_next(step, carry):
+            piece = in_order(step)
+
+            @pl.when(piece >= quarters)
+            def _():
+                wait_states(piece)
+
+            analyse(piece)
+
+            @pl.when(step >= LAG)
+            def _():
+                settle(in_order(step - LAG))
+
             return carry
 
-        lax.fori_loop(0, quarters, wait_top, 0)
-        spread_weights(weights_of(partial_sums()))
-
-        def analyse_top(piece, carry):
-            analyse(piece)
-            return carry
-
-        def analyse_next(piece, carry):
-            wait_states(piece)
-            analyse(piece)
-            return carry
-
-        lax.fori_loop(0, quarters, analyse_top, 0)
-        lax.fori_loop(quarters, pieces, analyse_next, 0)
+        lax.fori_loop(0, pieces, analyse_next, 0)
 
     @pl.when(outer)
     def _():
-        def take(piece, carry):
+        def take(step, carry):
+            piece = in_order(step)
             result_copy(piece).wait_recv()
             for store in stores(piece):
                 store.start()
+
+            @pl.when(step >= LAG)
+            def _():
+                settle(in_order(step - LAG))
+
             return carry
 
         lax.fori_loop(0, pieces, take, 0)
 
-    def finish_level(level, carry):
-        @pl.when(tile < tiles - 1)
-        def _():
-            halo_up(level).wait_send()
-
-        @pl.when(tile > 0)
-        def _():
-            halo_down(level).wait_send()
-
+    def finish(step, carry):
+        settle(in_order(step))
         return carry
 
-    lax.fori_loop(0, levels, finish_level, 0)
-
-    def finish(piece, carry):
-        state_copy(piece, across, 0).wait_send()
-
-        @pl.when(outer)
-        def _():
-            state_copy(piece, near, 1).wait_send()
-
-        @pl.when(inner)
-        def _():
-            result_copy(piece).wait_send()
-
-        for store in stores(piece):
-            store.wait()
-        return carry
-
-    lax.fori_loop(0, pieces, finish, 0)
+    lax.fori_loop(pieces - LAG, pieces, finish, 0)
 
 
 def on_device(
@@ -577,20 +792,37 @@
     pieces = levels * quarters
     count = obs_cell.shape[0]
     obs_rows = (count // cols, cols)
-    vmem = pl.BlockSpec(memory_space=pltpu.VMEM)
+    pinned = pl.BlockSpec(memory_space=pltpu.HBM)
     anywhere = pl.BlockSpec(memory_space=pl.ANY)
     dma = pltpu.SemaphoreType.DMA
-    result = pl.pallas_call(
+    operands = (
+        tracers,
+        horiz_mix,
+        vert_mix,
+        sunlit.reshape(-1, cols),
+        interaction,
+        remin.reshape(1, ntr),
+        obs_cell.reshape(obs_rows),
+        obs_tile.reshape(obs_rows),
+        obs_value.reshape(obs_rows),
+        obs_noise,
+        obs_var.reshape(obs_rows),
+    )
+    operands = [pltpu.with_memory_space_constraint(value, pltpu.HBM) for value in operands]
+    return pl.pallas_call(
         functools.partial(kernel, (tiles, mids, deeps)),
         out_shape=jax.ShapeDtypeStruct(tracers.shape, F32),
-        in_specs=[pl.BlockSpec(memory_space=pltpu.SMEM), anywhere] + [vmem] * 9,
+        in_specs=[pinned] * len(operands),
         out_specs=anywhere,
         scratch_shapes=[
+            *[pltpu.VMEM(value.shape, value.dtype) for value in operands[1:]],
+            pltpu.VMEM((rows, cols), F32),
+            pltpu.VMEM((pair, ntr, cols), F32),
             pltpu.VMEM((levels, rows + 2, pair, ntr, cols), F32),
             pltpu.VMEM((levels, rows, pair, ntr, cols), F32),
             pltpu.VMEM((levels, quarters, 8, QROWS, ntr, cols), F32),
-            pltpu.VMEM((pieces, pair, QROWS, ntr, cols), F32),
-            pltpu.VMEM((pieces, pair, QROWS, ntr, cols), F32),
+            pltpu.VMEM((pieces, QROWS, pair, ntr, cols), F32),
+            pltpu.VMEM((pieces, QROWS, pair, ntr, cols), F32),
             pltpu.VMEM((rows * 8, cols), F32),
             pltpu.VMEM((mids, deeps, GROUP, 128), F32),
             pltpu.VMEM((mids, deeps, GROUP, 128), F32),
@@ -599,14 +831,17 @@
             pltpu.VMEM((GROUP, 128), F32),
             pltpu.VMEM((GROUP, GROUP, 128), F32),
             pltpu.VMEM((4, 8, 8, 128), F32),
-            dma((levels, rows, pair)),
+            dma((10,)),
+            dma((levels, rows)),
+            dma,
+            dma,
             dma((levels, 2)),
             dma((levels, 2)),
             dma((pieces, 2)),
             dma((pieces, 4)),
             dma((pieces,)),
             dma((pieces,)),
-            dma((pieces, pair, QROWS)),
+            dma((pieces, QROWS)),
             dma((mids,)),
             dma((mids,)),
             dma((deeps,)),
@@ -615,26 +850,13 @@
             dma((GROUP,)),
         ],
         compiler_params=pltpu.CompilerParams(
-            collective_id=0, has_side_effects=True, vmem_limit_bytes=56 * 1024 * 1024
+            collective_id=0, has_side_effects=True, vmem_limit_bytes=VMEM_BYTES
         ),
         cost_estimate=pl.CostEstimate(
             flops=500_000_000, bytes_accessed=8_000_000, transcendentals=3_000_000
         ),
         name="step_and_analysis",
-    )(
-        sunlit,
-        tracers,
-        horiz_mix,
-        vert_mix,
-        split_coefficients(interaction),
-        remin.reshape(ntr, 1),
-        obs_cell.reshape(obs_rows),
-        obs_tile.reshape(obs_rows),
-        obs_value.reshape(obs_rows),
-        obs_noise,
-        obs_var.reshape(obs_rows),
-    )
-    return result
+    )(*operands)
 
 
 def solution(mesh):

time: 169 us -> 155 us (0.917); the launches traced: 166 us -> 154 us
  Pallas kernels: 160 us -> 153 us
  local copies, waits for them, and re-layouts: 5.31 us -> 1.67 us
    pallas_call x1, Pallas kernels: 160 us -> 153 us  [on_device(): pl.pallas_call(functools.partial(kernel, (tiles, mids, deeps)), out_shape...]
    unnamed x1, local copies, waits for them, and re-layouts: 3.97 us -> 1.67 us
where the time goes in v2:
time: 155 us; the launch traced here: 154 us
  Pallas kernels  153 us (99%)
  local copies, waits for them, and re-layouts  1.67 us (1%)
    pallas_call x1, Pallas kernels, on_device(): pl.pallas_call(functools.partial(kernel, (tiles, mids, deeps)), out_shape...  153 us

profile of v2, /device:TPU:224, one launch (start us, length us, event | category | flops | bytes accessed | tf_op | source)
XLA Modules:
  0.0 154.2 jit_solution(3102578580181000724)
XLA Ops:
  0.0 152.5 %step_and_analysis.1 = f32[2,48,8,8,128]{4,3,2,1,0:T(8,128)S(1)} custom-call(f32[2,48,8,8,128]{4,3,2,1,0:T(8,128)} %tracers.1, f32[8,8,128]{2,1,0:T(8,128)} %horiz_from.1, f32[7,8,128]{2,1,0:T(8,128)} %vert_from.1, s32[4,128]{1,0:T(4,128)} %bitcast.10, f32[48,48]{1,0:T(8,128)} %interaction_from.1, f32[1,48]{1,0:T(1,128)} %bitcast.11, s32[32,128]{1,0:T(8,128)} %bitcast.6, ...), custom_call_target="tpu_custom_call" | custom-call | flops 500000000 | bytes 8000000 | tf_op jit(solution)/shard_map/step_and_analysis/pallas_call | solution.py:812
  152.5 1.7 %copy.13 = f32[2,48,8,8,128]{4,3,2,1,0:T(8,128)} copy(f32[2,48,8,8,128]{4,3,2,1,0:T(8,128)S(1)} %step_and_analysis.1) | data formatting | bytes 6291456

commit v3 on v2

--- a/solution.py
+++ b/solution.py
@@ -11,7 +11,6 @@
 GROUP = 8
 DEEP = 2
 QROWS = 2
-LAG = 2
 VMEM_BYTES = 34 * 1024 * 1024
 OBS_STEP = 512
 F32 = jnp.float32
@@ -53,28 +52,25 @@
     surface,
     partial,
     recv_mid,
-    held_mid,
-    recv_deep,
     held_group,
     recv_group,
+    held_deep,
+    recv_deep,
     splats,
     small_sem,
     load_sem,
+    edge_sem,
     relay_send,
     relay_recv,
     halo_send,
     halo_recv,
     state_send,
-    state_recv,
+    piece_recv,
     result_send,
-    result_recv,
     store_sem,
-    mid_send,
-    mid_recv,
-    deep_send,
-    deep_recv,
-    group_send,
-    group_recv,
+    mid_sem,
+    group_sem,
+    deep_sem,
 ):
     tiles, mids, deeps = sizes
     ntr, levels, rows, cols = tracers.shape[1:]
@@ -89,6 +85,11 @@
     mid_at = lax.rem(tile // GROUP, mids)
     deep_at = tile // (GROUP * mids)
     half = tiles // 2
+    even = lax.rem(tile, 2) == 0
+    other_half = lax.rem(tile + half, tiles)
+    linked_up, linked_down = tile < tiles - 1, tile > 0
+    if deeps > 1:
+        linked_up, linked_down = linked_up & (tile != half - 1), linked_down & (tile != half)
     is_up_relay = (tile < half) & (lax.rem(tile, 4) == 2)
     is_down_relay = (tile >= half) & (lax.rem(tile, 4) == 1)
 
@@ -105,16 +106,11 @@
     def mid_tile(j):
         return (deep_at * mids + lax.rem(mid_at + j, mids)) * GROUP + group_at
 
-    def deep_tile(j):
-        return (lax.rem(deep_at + j, deeps) * mids + mid_at) * GROUP + group_at
-
     def group_tile(j):
         return (deep_at * mids + mid_at) * GROUP + lax.rem(group_at + j, GROUP)
 
-    def load(level, row):
-        return pltpu.make_async_copy(
-            tracers.at[:, :, level, row], raw.at[level, row + 1], load_sem.at[level, row]
-        )
+    def load(level, row, sem):
+        return pltpu.make_async_copy(tracers.at[:, :, level, row], raw.at[level, row + 1], sem)
 
     barrier = pltpu.get_barrier_semaphore()
     for j in range(1, 4):
@@ -122,11 +118,11 @@
             barrier, 1, device_id=(lax.rem(me + j, 4), tile), device_id_type=MESH
         )
 
-    @pl.when(tile > 0)
+    @pl.when(linked_down)
     def _():
         pl.semaphore_signal(barrier, 1, device_id=(me, tile - 1), device_id_type=MESH)
 
-    @pl.when(tile < tiles - 1)
+    @pl.when(linked_up)
     def _():
         pl.semaphore_signal(barrier, 1, device_id=(me, tile + 1), device_id_type=MESH)
 
@@ -134,12 +130,14 @@
     def _():
         for j in range(1, mids):
             pl.semaphore_signal(barrier, 1, device_id=(me, mid_tile(j)), device_id_type=MESH)
-        for j in range(1, deeps):
-            pl.semaphore_signal(barrier, 1, device_id=(me, deep_tile(j)), device_id_type=MESH)
         for j in range(1, GROUP):
             pl.semaphore_signal(barrier, 1, device_id=(me, group_tile(j)), device_id_type=MESH)
 
     if deeps > 1:
+
+        @pl.when(inner & even)
+        def _():
+            pl.semaphore_signal(barrier, 1, device_id=(me, other_half), device_id_type=MESH)
 
         @pl.when(tile == half - 1)
         def _():
@@ -183,12 +181,12 @@
 
     def start_middle(level, carry):
         for row in range(1, rows - 1):
-            load(level, row).start()
+            load(level, row, load_sem.at[level]).start()
         return carry
 
     def start_edges(level, carry):
-        for row in (0, rows - 1):
-            load(level, row).start()
+        for end in range(2):
+            load(level, end * (rows - 1), edge_sem.at[level, end]).start()
         return carry
 
     lax.fori_loop(0, 2, start_middle, 0)
@@ -197,7 +195,7 @@
         return pltpu.make_async_remote_copy(
             src_ref=raw.at[level, rows],
             dst_ref=raw.at[level, 0],
-            send_sem=halo_send.at[level, 0],
+            send_sem=halo_send.at[0],
             recv_sem=halo_recv.at[level, 0],
             device_id=(me, lax.rem(tile + 1, tiles)),
             device_id_type=MESH,
@@ -207,7 +205,7 @@
         return pltpu.make_async_remote_copy(
             src_ref=raw.at[level, 1],
             dst_ref=raw.at[level, rows + 1],
-            send_sem=halo_send.at[level, 1],
+            send_sem=halo_send.at[1],
             recv_sem=halo_recv.at[level, 1],
             device_id=(me, lax.rem(tile + tiles - 1, tiles)),
             device_id_type=MESH,
@@ -217,7 +215,7 @@
         return pltpu.make_async_remote_copy(
             src_ref=raw.at[level, row],
             dst_ref=relayed,
-            send_sem=halo_send.at[level, way],
+            send_sem=halo_send.at[way],
             recv_sem=relay_recv,
             device_id=(me, at),
             device_id_type=MESH,
@@ -256,14 +254,14 @@
             from_relay((tile - half) // 4, rows + 1, 1, half - 1).wait_send()
 
     def send_edges(level, carry):
-        for row in (0, rows - 1):
-            load(level, row).wait()
-
-        @pl.when((tile < tiles - 1) & (tile != half - 1))
+        for end in range(2):
+            load(level, end * (rows - 1), edge_sem.at[level, end]).wait()
+
+        @pl.when(linked_up)
         def _():
             halo_up(level).start()
 
-        @pl.when((tile > 0) & (tile != half))
+        @pl.when(linked_down)
         def _():
             halo_down(level).start()
 
@@ -291,8 +289,8 @@
             mixed[level, row, m] = own + strength * laplace
 
     def mix_middle(level):
-        for row in range(1, rows - 1):
-            load(level, row).wait()
+        middle = raw.at[level, pl.ds(2, rows - 2)]
+        pltpu.make_async_copy(middle, middle, load_sem.at[level]).wait()
 
         def mix_one(row, carry):
             mix_row(level, row)
@@ -330,8 +328,8 @@
         return pltpu.make_async_remote_copy(
             src_ref=block,
             dst_ref=block,
-            send_sem=state_send.at[piece, which],
-            recv_sem=state_recv.at[piece, me],
+            send_sem=state_send.at[which],
+            recv_sem=piece_recv.at[piece],
             device_id=(to, tile),
             device_id_type=MESH,
         )
@@ -409,9 +407,10 @@
     mix_middle(1)
     grow(0, 1)
 
-    peers = 3 + (tile > 0).astype(jnp.int32) + (tile < tiles - 1).astype(jnp.int32)
-    peers += jnp.where(inner, mids + deeps + GROUP - 3, 0)
+    peers = 3 + linked_up.astype(jnp.int32) + linked_down.astype(jnp.int32)
+    peers += jnp.where(inner, mids + GROUP - 2, 0)
     if deeps > 1:
+        peers += (inner & even).astype(jnp.int32)
         peers += (is_up_relay | is_down_relay).astype(jnp.int32)
         peers += jnp.where((tile == half - 1) | (tile == half), levels, 0)
     pl.semaphore_wait(barrier, peers)
@@ -465,26 +464,36 @@
         ending = step - (pieces - 2)
         return jnp.where(ending < 0, piece, (levels - 1) * quarters + 3 * ending)
 
+    def sent(source, sem):
+        pltpu.make_async_remote_copy(
+            src_ref=source,
+            dst_ref=source,
+            send_sem=sem,
+            recv_sem=sem,
+            device_id=(3 - me, tile),
+            device_id_type=MESH,
+        ).wait_send()
+
+    def landed(target, sem):
+        pltpu.make_async_remote_copy(
+            src_ref=target,
+            dst_ref=target,
+            send_sem=sem,
+            recv_sem=sem,
+            device_id=(3 - me, tile),
+            device_id_type=MESH,
+        ).wait_recv()
+
     def wait_states(piece):
         level, quarter = piece // quarters, lax.rem(piece, quarters)
-        for j in range(1, 4):
-            source = lax.rem(me + j, 4)
-            block = states.at[level, quarter, pl.ds(2 * source, 2)]
-            pltpu.make_async_remote_copy(
-                src_ref=block,
-                dst_ref=block,
-                send_sem=state_send.at[piece, 0],
-                recv_sem=state_recv.at[piece, source],
-                device_id=(source, tile),
-                device_id_type=MESH,
-            ).wait_recv()
+        landed(states.at[level, quarter, pl.ds(0, members - pair)], piece_recv.at[piece])
 
     def result_copy(piece):
         return pltpu.make_async_remote_copy(
             src_ref=passed.at[piece],
             dst_ref=results.at[piece],
-            send_sem=result_send.at[piece],
-            recv_sem=result_recv.at[piece],
+            send_sem=result_send,
+            recv_sem=piece_recv.at[piece],
             device_id=(beside, tile),
             device_id_type=MESH,
         )
@@ -495,7 +504,7 @@
             pltpu.make_async_copy(
                 results.at[piece, r],
                 out.at[:, :, level, quarter * QROWS + r],
-                store_sem.at[piece, r],
+                store_sem,
             )
             for r in range(QROWS)
         ]
@@ -565,79 +574,56 @@
                 at = (d * mids + b) * GROUP
                 partial[b, d] = total[at : at + GROUP]
 
-        copies = []
-        for j in range(1, mids):
-            other = lax.rem(mid_at + j, mids)
-            copies.append(
+        sums = partial[mid_at]
+        if mids > 1:
+            for j in range(1, mids):
                 small_copy(
-                    partial.at[other],
+                    partial.at[lax.rem(mid_at + j, mids)],
                     recv_mid.at[mid_at],
-                    mid_send.at[j],
-                    mid_recv.at[mid_at],
+                    mid_sem.at[0],
+                    mid_sem.at[1],
                     mid_tile(j),
-                )
-            )
-        for copy in copies:
-            copy.start()
-        sums = partial[mid_at]
-        for j in range(1, mids):
-            other = lax.rem(mid_at + j, mids)
-            small_copy(
-                recv_mid.at[other],
-                recv_mid.at[other],
-                mid_send.at[j],
-                mid_recv.at[other],
-                mid_tile(j),
-            ).wait_recv()
-            sums = sums + recv_mid[other]
-        held_mid[...] = sums
-        for j in range(1, deeps):
-            other = lax.rem(deep_at + j, deeps)
-            copies.append(
-                small_copy(
-                    held_mid.at[other],
-                    recv_deep.at[deep_at],
-                    deep_send.at[j],
-                    deep_recv.at[deep_at],
-                    deep_tile(j),
-                )
-            )
-            copies[-1].start()
-        sums = held_mid[deep_at]
-        for j in range(1, deeps):
-            other = lax.rem(deep_at + j, deeps)
-            small_copy(
-                recv_deep.at[other],
-                recv_deep.at[other],
-                deep_send.at[j],
-                deep_recv.at[other],
-                deep_tile(j),
-            ).wait_recv()
-            sums = sums + recv_deep[other]
+                ).start()
+            landed(recv_mid.at[pl.ds(0, mids - 1)], mid_sem.at[1])
+            for j in range(1, mids):
+                sums = sums + recv_mid[lax.rem(mid_at + j, mids)]
         held_group[...] = sums
         for j in range(1, GROUP):
-            copies.append(
-                small_copy(
-                    held_group,
-                    recv_group.at[group_at],
-                    group_send.at[j],
-                    group_recv.at[group_at],
-                    group_tile(j),
-                )
-            )
-            copies[-1].start()
-        for j in range(1, GROUP):
-            other = lax.rem(group_at + j, GROUP)
             small_copy(
                 held_group,
-                recv_group.at[other],
-                group_send.at[j],
-                group_recv.at[other],
+                recv_group.at[group_at],
+                group_sem.at[0],
+                group_sem.at[1],
                 group_tile(j),
-            ).wait_recv()
-            sums = sums + recv_group[other]
-        for copy in copies:
-            copy.wait_send()
+            ).start()
+        landed(recv_group.at[pl.ds(0, GROUP - 1)], group_sem.at[1])
+        for j in range(1, GROUP):
+            sums = sums + recv_group[lax.rem(group_at + j, GROUP)]
+        if mids > 1:
+            sent(partial.at[pl.ds(0, mids - 1)], mid_sem.at[0])
+        sent(recv_group.at[pl.ds(0, GROUP - 1)], group_sem.at[0])
+        if deeps == 1:
+            return sums[0]
+        held_deep[...] = sums
+        across_half = small_copy(
+            held_deep.at[1 - deep_at], recv_deep, deep_sem.at[0], deep_sem.at[1], other_half
+        )
+        handed = small_copy(
+            recv_deep, recv_deep, deep_sem.at[0], deep_sem.at[1], jnp.minimum(tile + 1, tiles - 1)
+        )
+
+        @pl.when(even)
+        def _():
+            across_half.start()
+            across_half.wait()
+            handed.start()
+            handed.wait_send()
+
+        @pl.when(jnp.logical_not(even))
+        def _():
+            handed.wait_recv()
+
+        sums = held_deep[deep_at] + recv_deep[...]
         return sums
 
     def weights_of(sums):
@@ -692,32 +678,16 @@
         for store in stores(piece):
             store.start()
 
-    def settle(piece):
-        state_copy(piece, across, 0).wait_send()
-
-        @pl.when(outer)
-        def _():
-            state_copy(piece, near, 1).wait_send()
-
-        @pl.when(inner)
-        def _():
-            result_copy(piece).wait_send()
-
-        for store in stores(piece):
-            store.wait()
-
-    def finish_level(level, carry):
-        @pl.when(tile < tiles - 1)
-        def _():
-            halo_up(level).wait_send()
-
-        @pl.when(tile > 0)
-        def _():
-            halo_down(level).wait_send()
-
-        return carry
-
-    lax.fori_loop(0, levels, finish_level, 0)
+    own_states = states.at[:, :, pl.ds(2 * me, 2)]
+
+    @pl.when(tile < tiles - 1)
+    def _():
+        sent(raw.at[:, rows], halo_send.at[0])
+
+    @pl.when(tile > 0)
+    def _():
+        sent(raw.at[:, 1], halo_send.at[1])
+
     if deeps > 1:
         end_pass()
 
@@ -739,14 +709,11 @@
                 wait_states(piece)
 
             analyse(piece)
-
-            @pl.when(step >= LAG)
-            def _():
-                settle(in_order(step - LAG))
-
             return carry
 
         lax.fori_loop(0, pieces, analyse_next, 0)
+        sent(passed, result_send)
+        sent(own_states, state_send.at[0])
 
     @pl.when(outer)
     def _():
@@ -755,20 +722,13 @@
             result_copy(piece).wait_recv()
             for store in stores(piece):
                 store.start()
-
-            @pl.when(step >= LAG)
-            def _():
-                settle(in_order(step - LAG))
-
             return carry
 
         lax.fori_loop(0, pieces, take, 0)
-
-    def finish(step, carry):
-        settle(in_order(step))
-        return carry
-
-    lax.fori_loop(pieces - LAG, pieces, finish, 0)
+        sent(own_states, state_send.at[0])
+        sent(own_states, state_send.at[1])
+
+    pltpu.make_async_copy(results, results, store_sem).wait()
 
 
 def on_device(
@@ -827,27 +787,24 @@
             pltpu.VMEM((mids, deeps, GROUP, 128), F32),
             pltpu.VMEM((mids, deeps, GROUP, 128), F32),
             pltpu.VMEM((deeps, GROUP, 128), F32),
+            pltpu.VMEM((GROUP, deeps, GROUP, 128), F32),
             pltpu.VMEM((deeps, GROUP, 128), F32),
             pltpu.VMEM((GROUP, 128), F32),
-            pltpu.VMEM((GROUP, GROUP, 128), F32),
             pltpu.VMEM((4, 8, 8, 128), F32),
             dma((10,)),
-            dma((levels, rows)),
+            dma((levels,)),
+            dma((levels, 2)),
             dma,
             dma,
+            dma((2,)),
             dma((levels, 2)),
-            dma((levels, 2)),
-            dma((pieces, 2)),
-            dma((pieces, 4)),
+            dma((2,)),
             dma((pieces,)),
-            dma((pieces,)),
-            dma((pieces, QROWS)),
-            dma((mids,)),
-            dma((mids,)),
-            dma((deeps,)),
-            dma((deeps,)),
-            dma((GROUP,)),
-            dma((GROUP,)),
+            dma,
+            dma,
+            dma((2,)),
+            dma((2,)),
+            dma((2,)),
         ],
         compiler_params=pltpu.CompilerParams(
             collective_id=0, has_side_effects=True, vmem_limit_bytes=VMEM_BYTES

time: 155 us -> 151 us (0.974)
  Pallas kernels: 153 us -> 149 us
    pallas_call x1, Pallas kernels: 153 us -> 149 us  [on_device(): pl.pallas_call(functools.partial(kernel, (tiles, mids, deeps)), out_shape...]
where the time goes in v3:
time: 151 us
  Pallas kernels  149 us (99%)
  local copies, waits for them, and re-layouts  1.67 us (1%)
    pallas_call x1, Pallas kernels, on_device(): pl.pallas_call(functools.partial(kernel, (tiles, mids, deeps)), out_shape...  149 us

profile of v3, /device:TPU:224, one launch (start us, length us, event | category | flops | bytes accessed | tf_op | source)
XLA Modules:
  0.0 150.8 jit_solution(16251592899649388434)
XLA Ops:
  0.0 149.2 %step_and_analysis.1 = f32[2,48,8,8,128]{4,3,2,1,0:T(8,128)S(1)} custom-call(f32[2,48,8,8,128]{4,3,2,1,0:T(8,128)} %tracers.1, f32[8,8,128]{2,1,0:T(8,128)} %horiz_from.1, f32[7,8,128]{2,1,0:T(8,128)} %vert_from.1, s32[4,128]{1,0:T(4,128)} %bitcast.10, f32[48,48]{1,0:T(8,128)} %interaction_from.1, f32[1,48]{1,0:T(1,128)} %bitcast.11, s32[32,128]{1,0:T(8,128)} %bitcast.6, ...), custom_call_target="tpu_custom_call" | custom-call | flops 500000000 | bytes 8000000 | tf_op jit(solution)/shard_map/step_and_analysis/pallas_call | solution.py:772
  149.2 1.7 %copy.13 = f32[2,48,8,8,128]{4,3,2,1,0:T(8,128)} copy(f32[2,48,8,8,128]{4,3,2,1,0:T(8,128)S(1)} %step_and_analysis.1) | data formatting | bytes 6291456

commit v4 on v3

--- a/solution.py
+++ b/solution.py
@@ -10,6 +10,8 @@
 NSUB = 4
 GROUP = 8
 DEEP = 2
+TAIL = 2
+AHEAD = 9
 QROWS = 2
 VMEM_BYTES = 34 * 1024 * 1024
 OBS_STEP = 512
@@ -57,6 +59,9 @@
     held_deep,
     recv_deep,
     splats,
+    splats_across,
+    tail_out,
+    tail_in,
     small_sem,
     load_sem,
     edge_sem,
@@ -68,6 +73,8 @@
     piece_recv,
     result_send,
     store_sem,
+    tail_sem,
+    tail_recv,
     mid_sem,
     group_sem,
     deep_sem,
@@ -77,6 +84,7 @@
     pair, quarters = 2, rows // QROWS
     members = 8
     pieces = levels * quarters
+    steps = pieces - TAIL
     me = lax.axis_index("member")
     tile = lax.axis_index("space")
     inner = (me == 1) | (me == 2)
@@ -387,9 +395,10 @@
                 at = (r * pair + m) * cols
                 states[level, quarter, 2 * me + m, r] = value[:, at : at + cols]
 
-    def send(level, quarter):
+    def send(level, quarter, whole=True):
         piece = level * quarters + quarter
-        state_copy(piece, across, 0).start()
+        if whole:
+            state_copy(piece, across, 0).start()
 
         @pl.when(outer)
         def _():
@@ -426,7 +435,7 @@
 
     for quarter in range(1, quarters - 1):
         grow(1, quarter)
-        send(1, quarter)
+        send(1, quarter, whole=False)
     if deeps > 1:
         pass_on()
     mix_edges(0)
@@ -455,13 +464,14 @@
         send(levels - 1, quarter)
 
     def in_order(step):
-        later = step - 2
-        level, turn = 1 + later // 4, lax.rem(later, 4)
+        later = step - 4
+        level, turn = 2 + later // 4, lax.rem(later, 4)
         piece = jnp.where(
             turn < 2, level * quarters + 1 + turn, (level - 1) * quarters + 3 * (turn - 2)
         )
+        piece = jnp.where(step < 4, 3 * (step - 2), piece)
         piece = jnp.where(step < 2, 1 + step, piece)
-        ending = step - (pieces - 2)
+        ending = step - (steps - 2)
         return jnp.where(ending < 0, piece, (levels - 1) * quarters + 3 * ending)
 
     def sent(source, sem):
@@ -657,6 +667,66 @@
             for k in range(members):
                 splats[j, k] = jnp.broadcast_to(wide[k : k + 1], (8, 128))
 
+        for j in range(4):
+            member = 2 * across + j if j < 2 else 2 * (3 - beside) + j - 2
+            column = jnp.sum(
+                jnp.where(lane8 == members + member, centered, 0.0), axis=1, keepdims=True
+            )
+            wide = jnp.broadcast_to(column, (8, 128))
+            for k in range(4):
+                source = 2 * me + k if k < 2 else 2 * beside + k - 2
+                row = jnp.sum(jnp.where(sub == source, wide, 0.0), axis=0, keepdims=True)
+                splats_across[j, k] = jnp.broadcast_to(row, (8, 128))
+
+    def tail_piece(at):
+        return quarters + 1 + at
+
+    def tail_copy(at, to, which):
+        return pltpu.make_async_remote_copy(
+            src_ref=tail_out.at[at, which],
+            dst_ref=tail_in.at[at],
+            send_sem=tail_sem,
+            recv_sem=tail_recv.at[at],
+            device_id=(to, tile),
+            device_id_type=MESH,
+        )
+
+    def analyse_tail(at):
+        piece = tail_piece(at)
+        level, quarter = 1, 1 + at
+        near_states = states.at[level, quarter, pl.ds(0, pair)]
+        landed(near_states, piece_recv.at[piece])
+
+        def tail_part(part, carry):
+            r, first = part // (ntr // 8), pl.multiple_of(lax.rem(part, ntr // 8) * 8, 8)
+            values = [
+                states[level, quarter, 2 * source + k, r, pl.ds(first, 8), :]
+                for source in (me, beside)
+                for k in range(pair)
+            ]
+            for j in range(4):
+                same_side, other_side = None, None
+                for k in range(4):
+                    source = 2 * me + k if k < 2 else 2 * beside + k - 2
+                    here = values[k] * splats[j, source]
+                    there = values[k] * splats_across[j, k]
+                    same_side = here if k == 0 else same_side + here
+                    other_side = there if k == 0 else other_side + there
+                target = results if j < 2 else passed
+                target[piece, r, j % 2, pl.ds(first, 8), :] = same_side
+                tail_out[at, j // 2, r, j % 2, pl.ds(first, 8), :] = other_side
+            return carry
+
+        lax.fori_loop(0, QROWS * (ntr // 8), tail_part, 0)
+        result_copy(piece).start()
+
+    def finish_tail(at):
+        piece = tail_piece(at)
+        landed(tail_in.at[at], tail_recv.at[at])
+        results[piece] = results[piece] + tail_in[at]
+        for store in stores(piece):
+            store.start()
+
     def analyse(piece):
         level, quarter = piece // quarters, lax.rem(piece, quarters)
 
@@ -700,6 +770,8 @@
         for quarter in (0, quarters - 1):
             wait_states(quarter)
         spread_weights(weights_of(partial_sums()))
+        for at in range(TAIL):
+            analyse_tail(at)
 
         def analyse_next(step, carry):
             piece = in_order(step)
@@ -709,11 +781,21 @@
                 wait_states(piece)
 
             analyse(piece)
+
+            @pl.when(step == steps - AHEAD)
+            def _():
+                for at in range(TAIL):
+                    tail_copy(at, 3 - beside, 1).start()
+                    tail_copy(at, across, 0).start()
+
             return carry
 
-        lax.fori_loop(0, pieces, analyse_next, 0)
+        lax.fori_loop(0, steps, analyse_next, 0)
+        for at in range(TAIL):
+            finish_tail(at)
+        sent(tail_out, tail_sem)
         sent(passed, result_send)
-        sent(own_states, state_send.at[0])
+        sent(passed.at[pl.ds(0, steps)], state_send.at[0])
 
     @pl.when(outer)
     def _():
@@ -724,8 +806,11 @@
                 store.start()
             return carry
 
-        lax.fori_loop(0, pieces, take, 0)
-        sent(own_states, state_send.at[0])
+        lax.fori_loop(0, steps, take, 0)
+        for at in range(TAIL):
+            result_copy(tail_piece(at)).wait_recv()
+            finish_tail(at)
+        sent(passed.at[pl.ds(0, steps)], state_send.at[0])
         sent(own_states, state_send.at[1])
 
     pltpu.make_async_copy(results, results, store_sem).wait()
@@ -791,6 +876,9 @@
             pltpu.VMEM((deeps, GROUP, 128), F32),
             pltpu.VMEM((GROUP, 128), F32),
             pltpu.VMEM((4, 8, 8, 128), F32),
+            pltpu.VMEM((4, 4, 8, 128), F32),
+            pltpu.VMEM((TAIL, 2, QROWS, pair, ntr, cols), F32),
+            pltpu.VMEM((TAIL, QROWS, pair, ntr, cols), F32),
             dma((10,)),
             dma((levels,)),
             dma((levels, 2)),
@@ -802,6 +890,8 @@
             dma((pieces,)),
             dma,
             dma,
+            dma,
+            dma((TAIL,)),
             dma((2,)),
             dma((2,)),
             dma((2,)),

time: 151 us -> 147 us (0.974)
  Pallas kernels: 149 us -> 145 us
    pallas_call x1, Pallas kernels: 149 us -> 145 us  [on_device(): pl.pallas_call(functools.partial(kernel, (tiles, mids, deeps)), out_shape...]
where the time goes in v4:
time: 147 us
  Pallas kernels  145 us (99%)
  local copies, waits for them, and re-layouts  1.67 us (1%)
    pallas_call x1, Pallas kernels, on_device(): pl.pallas_call(functools.partial(kernel, (tiles, mids, deeps)), out_shape...  145 us

profile of v4, /device:TPU:224, one launch (start us, length us, event | category | flops | bytes accessed | tf_op | source)
XLA Modules:
  0.0 146.9 jit_solution(8147387850803119264)
XLA Ops:
  0.0 145.2 %step_and_analysis.1 = f32[2,48,8,8,128]{4,3,2,1,0:T(8,128)S(1)} custom-call(f32[2,48,8,8,128]{4,3,2,1,0:T(8,128)} %tracers.1, f32[8,8,128]{2,1,0:T(8,128)} %horiz_from.1, f32[7,8,128]{2,1,0:T(8,128)} %vert_from.1, s32[4,128]{1,0:T(4,128)} %bitcast.10, f32[48,48]{1,0:T(8,128)} %interaction_from.1, f32[1,48]{1,0:T(1,128)} %bitcast.11, s32[32,128]{1,0:T(8,128)} %bitcast.6, ...), custom_call_target="tpu_custom_call" | custom-call | flops 500000000 | bytes 8000000 | tf_op jit(solution)/shard_map/step_and_analysis/pallas_call | solution.py:857
  145.2 1.7 %copy.13 = f32[2,48,8,8,128]{4,3,2,1,0:T(8,128)} copy(f32[2,48,8,8,128]{4,3,2,1,0:T(8,128)S(1)} %step_and_analysis.1) | data formatting | bytes 6291456

commit v5 on v4

--- a/solution.py
+++ b/solution.py
@@ -10,7 +10,8 @@
 NSUB = 4
 GROUP = 8
 DEEP = 2
-TAIL = 2
+TAIL_LEVELS = 2
+TAIL = 2 * TAIL_LEVELS
 AHEAD = 9
 QROWS = 2
 VMEM_BYTES = 34 * 1024 * 1024
@@ -397,7 +398,8 @@
 
     def send(level, quarter, whole=True):
         piece = level * quarters + quarter
-        if whole:
+        @pl.when(whole)
+        def _():
             state_copy(piece, across, 0).start()
 
         @pl.when(outer)
@@ -451,7 +453,7 @@
 
         for quarter in range(1, quarters - 1):
             grow(level, quarter)
-            send(level, quarter)
+            send(level, quarter, whole=level > TAIL_LEVELS)
         mix_edges(level)
         for quarter in (0, quarters - 1):
             grow(level - 1, quarter)
@@ -464,12 +466,15 @@
         send(levels - 1, quarter)
 
     def in_order(step):
-        later = step - 4
-        level, turn = 2 + later // 4, lax.rem(later, 4)
+        edge = step - 2
+        later = edge - TAIL
+        level, turn = TAIL_LEVELS + 1 + later // 4, lax.rem(later, 4)
         piece = jnp.where(
             turn < 2, level * quarters + 1 + turn, (level - 1) * quarters + 3 * (turn - 2)
         )
-        piece = jnp.where(step < 4, 3 * (step - 2), piece)
+        piece = jnp.where(
+            edge < TAIL, edge // 2 * quarters + 3 * lax.rem(edge, 2), piece
+        )
         piece = jnp.where(step < 2, 1 + step, piece)
         ending = step - (steps - 2)
         return jnp.where(ending < 0, piece, (levels - 1) * quarters + 3 * ending)
@@ -679,7 +684,7 @@
                 splats_across[j, k] = jnp.broadcast_to(row, (8, 128))
 
     def tail_piece(at):
-        return quarters + 1 + at
+        return (1 + at // 2) * quarters + 1 + at % 2
 
     def tail_copy(at, to, which):
         return pltpu.make_async_remote_copy(
@@ -693,7 +698,7 @@
 
     def analyse_tail(at):
         piece = tail_piece(at)
-        level, quarter = 1, 1 + at
+        level, quarter = 1 + at // 2, 1 + at % 2
         near_states = states.at[level, quarter, pl.ds(0, pair)]
         landed(near_states, piece_recv.at[piece])
 

time: 147 us -> 145 us (0.986)
  Pallas kernels: 145 us -> 142 us
    pallas_call x1, Pallas kernels: 145 us -> 142 us  [on_device(): pl.pallas_call(functools.partial(kernel, (tiles, mids, deeps)), out_shape...]
where the time goes in v5:
time: 145 us; the launch traced here: 144 us
  Pallas kernels  142 us (98%)
  local copies, waits for them, and re-layouts  1.67 us (1%)
    pallas_call x1, Pallas kernels, on_device(): pl.pallas_call(functools.partial(kernel, (tiles, mids, deeps)), out_shape...  142 us

profile of v5, /device:TPU:224, one launch (start us, length us, event | category | flops | bytes accessed | tf_op | source)
XLA Modules:
  0.0 143.9 jit_solution(14175053133517746300)
XLA Ops:
  0.0 142.2 %step_and_analysis.1 = f32[2,48,8,8,128]{4,3,2,1,0:T(8,128)S(1)} custom-call(f32[2,48,8,8,128]{4,3,2,1,0:T(8,128)} %tracers.1, f32[8,8,128]{2,1,0:T(8,128)} %horiz_from.1, f32[7,8,128]{2,1,0:T(8,128)} %vert_from.1, s32[4,128]{1,0:T(4,128)} %bitcast.10, f32[48,48]{1,0:T(8,128)} %interaction_from.1, f32[1,48]{1,0:T(1,128)} %bitcast.11, s32[32,128]{1,0:T(8,128)} %bitcast.6, ...), custom_call_target="tpu_custom_call" | custom-call | flops 500000000 | bytes 8000000 | tf_op jit(solution)/shard_map/step_and_analysis/pallas_call | solution.py:862
  142.2 1.7 %copy.13 = f32[2,48,8,8,128]{4,3,2,1,0:T(8,128)} copy(f32[2,48,8,8,128]{4,3,2,1,0:T(8,128)S(1)} %step_and_analysis.1) | data formatting | bytes 6291456

commit v6 on v5

--- a/solution.py
+++ b/solution.py
@@ -791,6 +791,7 @@
             def _():
                 for at in range(TAIL):
                     tail_copy(at, 3 - beside, 1).start()
+                for at in range(TAIL):
                     tail_copy(at, across, 0).start()
 
             return carry

time: 145 us -> 145 us (level)
  no operation moved by 1% of the time
where the time goes in v6:
time: 145 us; the launch traced here: 143 us
  Pallas kernels  141 us (97%)
  local copies, waits for them, and re-layouts  1.67 us (1%)
    pallas_call x1, Pallas kernels, on_device(): pl.pallas_call(functools.partial(kernel, (tiles, mids, deeps)), out_shape...  141 us

profile of v6, /device:TPU:224, one launch (start us, length us, event | category | flops | bytes accessed | tf_op | source)
XLA Modules:
  0.0 142.8 jit_solution(11710125920925911055)
XLA Ops:
  0.0 141.1 %step_and_analysis.1 = f32[2,48,8,8,128]{4,3,2,1,0:T(8,128)S(1)} custom-call(f32[2,48,8,8,128]{4,3,2,1,0:T(8,128)} %tracers.1, f32[8,8,128]{2,1,0:T(8,128)} %horiz_from.1, f32[7,8,128]{2,1,0:T(8,128)} %vert_from.1, s32[4,128]{1,0:T(4,128)} %bitcast.10, f32[48,48]{1,0:T(8,128)} %interaction_from.1, f32[1,48]{1,0:T(1,128)} %bitcast.11, s32[32,128]{1,0:T(8,128)} %bitcast.6, ...), custom_call_target="tpu_custom_call" | custom-call | flops 500000000 | bytes 8000000 | tf_op jit(solution)/shard_map/step_and_analysis/pallas_call | solution.py:863
  141.1 1.7 %copy.13 = f32[2,48,8,8,128]{4,3,2,1,0:T(8,128)} copy(f32[2,48,8,8,128]{4,3,2,1,0:T(8,128)S(1)} %step_and_analysis.1) | data formatting | bytes 6291456

commit v7 on v6

--- a/solution.py
+++ b/solution.py
@@ -11,6 +11,7 @@
 GROUP = 8
 DEEP = 2
 TAIL_LEVELS = 2
+TAIL_FROM = 3
 TAIL = 2 * TAIL_LEVELS
 AHEAD = 9
 QROWS = 2
@@ -437,7 +438,7 @@
 
     for quarter in range(1, quarters - 1):
         grow(1, quarter)
-        send(1, quarter, whole=False)
+        send(1, quarter, whole=TAIL_FROM > 1)
     if deeps > 1:
         pass_on()
     mix_edges(0)
@@ -453,7 +454,7 @@
 
         for quarter in range(1, quarters - 1):
             grow(level, quarter)
-            send(level, quarter, whole=level > TAIL_LEVELS)
+            send(level, quarter, whole=(level < TAIL_FROM) | (level >= TAIL_FROM + TAIL_LEVELS))
         mix_edges(level)
         for quarter in (0, quarters - 1):
             grow(level - 1, quarter)
@@ -466,17 +467,15 @@
         send(levels - 1, quarter)
 
     def in_order(step):
-        edge = step - 2
-        later = edge - TAIL
-        level, turn = TAIL_LEVELS + 1 + later // 4, lax.rem(later, 4)
+        for turn in range(TAIL_LEVELS):
+            step = jnp.where(step >= 4 * (TAIL_FROM + turn) - 2, step + 2, step)
+        later = step - 2
+        level, turn = 1 + later // 4, lax.rem(later, 4)
         piece = jnp.where(
             turn < 2, level * quarters + 1 + turn, (level - 1) * quarters + 3 * (turn - 2)
         )
-        piece = jnp.where(
-            edge < TAIL, edge // 2 * quarters + 3 * lax.rem(edge, 2), piece
-        )
         piece = jnp.where(step < 2, 1 + step, piece)
-        ending = step - (steps - 2)
+        ending = step - (pieces - 2)
         return jnp.where(ending < 0, piece, (levels - 1) * quarters + 3 * ending)
 
     def sent(source, sem):
@@ -684,7 +683,7 @@
                 splats_across[j, k] = jnp.broadcast_to(row, (8, 128))
 
     def tail_piece(at):
-        return (1 + at // 2) * quarters + 1 + at % 2
+        return (TAIL_FROM + at // 2) * quarters + 1 + at % 2
 
     def tail_copy(at, to, which):
         return pltpu.make_async_remote_copy(
@@ -698,7 +697,7 @@
 
     def analyse_tail(at):
         piece = tail_piece(at)
-        level, quarter = 1 + at // 2, 1 + at % 2
+        level, quarter = TAIL_FROM + at // 2, 1 + at % 2
         near_states = states.at[level, quarter, pl.ds(0, pair)]
         landed(near_states, piece_recv.at[piece])
 

time: 145 us -> 145 us (level)
  no operation moved by 1% of the time
where the time goes in v7:
time: 145 us; the launch traced here: 143 us
  Pallas kernels  141 us (97%)
  local copies, waits for them, and re-layouts  1.67 us (1%)
    pallas_call x1, Pallas kernels, on_device(): pl.pallas_call(functools.partial(kernel, (tiles, mids, deeps)), out_shape...  141 us

profile of v7, /device:TPU:224, one launch (start us, length us, event | category | flops | bytes accessed | tf_op | source)
XLA Modules:
  0.0 142.9 jit_solution(15349335758820046847)
XLA Ops:
  0.0 141.2 %step_and_analysis.1 = f32[2,48,8,8,128]{4,3,2,1,0:T(8,128)S(1)} custom-call(f32[2,48,8,8,128]{4,3,2,1,0:T(8,128)} %tracers.1, f32[8,8,128]{2,1,0:T(8,128)} %horiz_from.1, f32[7,8,128]{2,1,0:T(8,128)} %vert_from.1, s32[4,128]{1,0:T(4,128)} %bitcast.10, f32[48,48]{1,0:T(8,128)} %interaction_from.1, f32[1,48]{1,0:T(1,128)} %bitcast.11, s32[32,128]{1,0:T(8,128)} %bitcast.6, ...), custom_call_target="tpu_custom_call" | custom-call | flops 500000000 | bytes 8000000 | tf_op jit(solution)/shard_map/step_and_analysis/pallas_call | solution.py:862
  141.2 1.7 %copy.13 = f32[2,48,8,8,128]{4,3,2,1,0:T(8,128)} copy(f32[2,48,8,8,128]{4,3,2,1,0:T(8,128)S(1)} %step_and_analysis.1) | data formatting | bytes 6291456
